TPU v7x, 32 devices: a whole 2x2x4 slice. The times are simulated.
32 devices in a mesh: groups: 1, dev: 8 (over z, y), side: 4 (over x, core).
Axes of the slice: x: 2, y: 2, z: 4, core: 2. Of those that a mesh axis runs over, the one named last changes fastest.
Arguments:
- queries: bfloat16 [256, 4096], P(('groups', 'dev', 'side')), may hold values from -160 to 160
- kv_cache: bfloat16 [256, 192, 1024], P(('groups', 'dev', 'side')), may hold values from -4 to 4
- new_kv: bfloat16 [256, 1024], P(('groups', 'dev', 'side')), may hold values from -4 to 4
- lengths: int32 [256], P(('groups', 'dev', 'side')), may hold values from 24 to 192, as said below
- residual: bfloat16 [256, 2048], P(('groups', 'dev', 'side')), may hold values from -36 to 36
- w_out: bfloat16 [4096, 2048], P('side'), may hold values from -0.59765625 to 0.59765625
- norm_gain: float32 [2048], replicated, may hold values from 0.5 to 1.5
- expert_ids: int32 [256, 8], P(('groups', 'dev', 'side')), may hold values from 0 to 15, all different within a row; in each aligned block of 8 rows (0 to 7, 8 to 15, ...) at most 8 rows name the same one
- route_level: int32 [256, 8], P(('groups', 'dev', 'side')), may hold values from 1 to 255
- w_in: bfloat16 [32, 2048, 768], P(('dev', 'side')), may hold values from -0.125 to 0.125
- w_down: bfloat16 [32, 384, 2048], P(('dev', 'side')), may hold values from -0.4375 to 0.4375
Outputs:
- stream: bfloat16 [256, 2048], P(('groups', 'dev', 'side'))
- expert_sum: bfloat16 [256, 2048], P(('groups', 'dev', 'side'))
Inputs may be any that keep to these rules, and one draw needn't show every extreme that they name: `lengths`: in each aligned block of 8 requests some request has 192 cached tokens. `expert_ids`: A row names 8 different experts. In each aligned block of 8 rows no expert is named by more than 8 rows, and in some block some expert is named by exactly 8 rows.
All inputs are finite; a program needn't handle non-finite values.
Results may differ from a plain program's by a relative error of at most 0.013.
Values may be sent and summed in bfloat16 or wider, within the bound.
A program may use at most 64 MiB of HBM per device.

v0:
```python
import math

import jax
import jax.numpy as jnp
from jax import lax
from jax.sharding import PartitionSpec as P

HQ = 32
KVH = 4
HD = 128
CACHE = 192


def partner(block, axis, bit):
    count = lax.axis_size(axis)
    route = []
    for low in range(count):
        high = low | 1 << bit
        if high != low and high < count:
            route += [(low, high), (high, low)]
    return lax.ppermute(block, axis, route)


def attend(queries, kv_cache, new_kv, lengths):
    req_rows = queries.shape[0]
    group_size = HQ // KVH
    split_at = KVH * HD
    grouped_q = queries.reshape(req_rows, KVH, group_size, HD)
    key_rows = kv_cache[:, :, :split_at].reshape(req_rows, CACHE, KVH, HD)
    value_rows = kv_cache[:, :, split_at:].reshape(req_rows, CACHE, KVH, HD)
    new_key = new_kv[:, :split_at].reshape(req_rows, KVH, HD)
    new_value = new_kv[:, split_at:].reshape(req_rows, KVH, HD)
    scaling = 1.0 / math.sqrt(HD)
    scores = (
        jnp.einsum("rgqd,rlgd->rgql", grouped_q, key_rows, preferred_element_type=jnp.float32)
        * scaling
    )
    own_score = (
        jnp.einsum("rgqd,rgd->rgq", grouped_q, new_key, preferred_element_type=jnp.float32)
        * scaling
    )
    visible = (jnp.arange(CACHE)[None, :] < lengths[:, None])[:, None, None, :]
    scores = jnp.where(visible, scores, -jnp.inf)
    peak = jnp.maximum(jnp.max(scores, axis=3), own_score)
    weights = jnp.where(visible, jnp.exp(scores - peak[..., None]), 0.0)
    own_weight = jnp.exp(own_score - peak)
    denominator = jnp.sum(weights, axis=3) + own_weight
    probability = (weights / denominator[..., None]).astype(jnp.bfloat16)
    own_prob = (own_weight / denominator).astype(jnp.bfloat16)
    mixed = jnp.einsum(
        "rgql,rlgd->rgqd", probability, value_rows, preferred_element_type=jnp.float32
    )
    mixed = (
        mixed
        + own_prob.astype(jnp.float32)[..., None] * new_value.astype(jnp.float32)[:, :, None, :]
    )
    return mixed.reshape(req_rows, HQ * HD).astype(jnp.bfloat16)


def expert_rows(received, gate_up_w, down_w):
    model_width = received.shape[2]
    flattened = received.reshape(-1, model_width)
    half_units = down_w.shape[0]
    gate_up = jnp.dot(flattened, gate_up_w, preferred_element_type=jnp.float32)
    hidden = (jax.nn.silu(gate_up[:, :half_units]) * gate_up[:, half_units:]).astype(jnp.bfloat16)
    result = jnp.dot(hidden, down_w, preferred_element_type=jnp.float32)
    return result.reshape(received.shape[0], received.shape[1], model_width)


def body(
    queries,
    kv_cache,
    new_kv,
    lengths,
    residual,
    w_out,
    norm_gain,
    expert_ids,
    route_level,
    w_in,
    w_down,
):
    req_rows = queries.shape[0]
    top_count = expert_ids.shape[1]
    model_width = residual.shape[1]
    attended = attend(queries, kv_cache, new_kv, lengths)
    columns = lax.all_to_all(attended, "side", split_axis=1, concat_axis=0, tiled=True)
    attention = lax.psum_scatter(
        jnp.dot(columns, w_out, preferred_element_type=jnp.float32),
        "side",
        scatter_dimension=0,
        tiled=True,
    )
    stream = residual.astype(jnp.float32) + attention
    mean_square = jnp.mean(stream * stream, axis=1, keepdims=True)
    normed = (stream * lax.rsqrt(mean_square + 1e-06) * norm_gain[None, :]).astype(jnp.bfloat16)
    shares = route_level.astype(jnp.float32)
    shares = shares / jnp.sum(shares, axis=1, keepdims=True)
    shards = lax.axis_size("dev") * lax.axis_size("side")
    experts = shards // 2
    capacity = 2 * req_rows * top_count // experts
    pair_expert = expert_ids.reshape(-1)
    one_hot = (pair_expert[:, None] == jnp.arange(experts, dtype=jnp.int32)[None, :]).astype(
        jnp.int32
    )
    slot_rank = jnp.sum((jnp.cumsum(one_hot, axis=0) - 1) * one_hot, axis=1)
    target = pair_expert * capacity + slot_rank
    placed = target[None, :] == jnp.arange(experts * capacity, dtype=jnp.int32)[:, None]
    placed = placed.reshape(experts * capacity, req_rows, top_count)
    picker = jnp.any(placed, axis=2).astype(jnp.bfloat16)
    mixing = jnp.sum(jnp.where(placed, shares[None, :, :], 0.0), axis=2).T
    outbox = jnp.dot(picker, normed, preferred_element_type=jnp.float32).astype(jnp.bfloat16)
    grouped = outbox.reshape(experts, capacity, model_width)
    pair_side = lax.axis_index("side") % 2
    gate_up_w = w_in[0]
    down_w = w_down[0]
    doubled = jnp.broadcast_to(grouped[:, None], (experts, 2, capacity, model_width))
    doubled = doubled.reshape(shards, capacity, model_width)
    partials = expert_rows(
        lax.all_to_all(doubled, ("dev", "side"), split_axis=0, concat_axis=0, tiled=True),
        gate_up_w,
        down_w,
    )
    halved = partials.reshape(shards, 2, capacity // 2, model_width)
    retained = jnp.where(pair_side == 0, halved[:, 0], halved[:, 1])
    handed = jnp.where(pair_side == 0, halved[:, 1], halved[:, 0])
    gained = partner(handed, "side", 0)
    joined = (retained + gained).astype(jnp.bfloat16)
    returned = lax.all_to_all(joined, ("dev", "side"), split_axis=0, concat_axis=0, tiled=True)
    outputs = returned.reshape(experts, capacity, model_width)
    expert_sum = jnp.dot(
        mixing,
        outputs.reshape(experts * capacity, model_width).astype(jnp.float32),
        precision=lax.Precision.HIGHEST,
    )
    return (stream.astype(jnp.bfloat16), expert_sum.astype(jnp.bfloat16))


def solution(mesh):
    return jax.shard_map(
        body,
        mesh=mesh,
        in_specs=(
            P(("groups", "dev", "side"), None),
            P(("groups", "dev", "side"), None, None),
            P(("groups", "dev", "side"), None),
            P(("groups", "dev", "side")),
            P(("groups", "dev", "side"), None),
            P("side", None),
            P(),
            P(("groups", "dev", "side"), None),
            P(("groups", "dev", "side"), None),
            P(("dev", "side"), None, None),
            P(("dev", "side"), None, None),
        ),
        out_specs=(P(("groups", "dev", "side"), None), P(("groups", "dev", "side"), None)),
        check_vma=False,
    )
```

profile of v0, /device:TPU:0, one launch (start us, length us, event | category | flops | bytes accessed | tf_op | source)
XLA Modules:
  0.0 120.9 jit_solution(14539800376660734263)
XLA Ops:
  7.2 0.9 iota_compare_fusion.2
  8.1 0.8 bitcast_convert_fusion
  8.9 2.5 %slice_bitcast_fusion.1 = (bf16[8,24,4,8,128]{4,3,2,1,0:T(8,128)(2,1)S(1)}, bf16[8,24,4,8,128]{4,3,2,1,0:T(8,128)(2,1)S(1)}) fusion(bf16[8,192,1024]{2,1,0:T(8,128)(2,1)} %param.12), kind=kLoop, calls=%fused_computation.14 | loop fusion | bytes 6291456
  11.5 1.0 fusion.46
  12.5 0.2 fusion.26
  12.8 0.6 fusion.20
  13.4 0.6 copy.34
  14.0 4.2 %all-to-all-start = ((bf16[8,4,1024]{2,0,1:T(8,128)(2,1)}), bf16[8,4,1024]{2,0,1:T(8,128)(2,1)S(1)}, u32[]{:S(2)}, u32[]{:S(2)}) async-start(bf16[8,4,1024]{2,0,1:T(8,128)(2,1)} %copy.34), calls=%async_computation | async-start | bytes 131072 | tf_op jit(solution)/shard_map/all_to_all | solution.py:87
  18.3 4.0 %all-to-all-done = bf16[8,4,1024]{2,0,1:T(8,128)(2,1)S(1)} async-done(((bf16[8,4,1024]{2,0,1:T(8,128)(2,1)}), bf16[8,4,1024]{2,0,1:T(8,128)(2,1)S(1)}, u32[]{:S(2)}, u32[]{:S(2)}) %all-to-all-start) | async-done | bytes 65568 | tf_op jit(solution)/shard_map/all_to_all | solution.py:87
  22.4 3.7 %fusion.32 = f32[32,2048]{1,0:T(8,128)} fusion(bf16[1024,2048]{1,0:T(8,128)(2,1)} %param.16, bf16[8,4,1024]{2,0,1:T(8,128)(2,1)S(1)} %all-to-all-done), kind=kOutput, calls=%fused_computation.33 | convolution fusion | flops 134217728 | bytes 4521984 | tf_op jit(solution)/shard_map/dot_general | solution.py:89
  26.7 20.5 %reduce-scatter.2.cloned.1.call-done = f32[8,2048]{1,0:T(8,128)} async-done(((f32[32,2048]{1,0:T(8,128)}), f32[8,2048]{1,0:T(8,128)}) %reduce-scatter.2.cloned.1.call-update) | async-done | bytes 65552 | tf_op jit(solution)/shard_map/reduce_scatter | solution.py:88
  47.1 1.6 %multiply_reduce_fusion = (f32[8]{0:T(128)S(1)}, bf16[8,2048]{1,0:T(8,128)(2,1)}) fusion(f32[8,2048]{1,0:T(8,128)} %reduce-scatter.2.cloned.1.call-done, bf16[8,2048]{1,0:T(8,128)(2,1)S(1)} %copy-done.1), kind=kLoop, calls=%fused_computation.36 | loop fusion | flops 81912 | bytes 131104 | tf_op jit(solution)/shard_map/reduce_sum | solution.py:95
  48.7 1.2 fusion.2
  49.9 1.2 broadcast_in_dim.57
  51.1 4.7 %all-to-all-start.1 = ((bf16[32,8,2048]{2,1,0:T(8,128)(2,1)}), bf16[32,8,2048]{2,1,0:T(8,128)(2,1)}, u32[]{:S(2)}, u32[]{:S(2)}) async-start(bf16[32,8,2048]{2,1,0:T(8,128)(2,1)} %bitcast.63), calls=%async_computation.2 | async-start | bytes 2097152 | tf_op jit(solution)/shard_map/all_to_all | solution.py:120
  55.9 26.2 %all-to-all-done.1 = bf16[32,8,2048]{2,1,0:T(8,128)(2,1)} async-done(((bf16[32,8,2048]{2,1,0:T(8,128)(2,1)}), bf16[32,8,2048]{2,1,0:T(8,128)(2,1)}, u32[]{:S(2)}, u32[]{:S(2)}) %all-to-all-start.1) | async-done | bytes 1048608 | tf_op jit(solution)/shard_map/all_to_all | solution.py:120
  82.1 2.2 %fusion = f32[256,768]{1,0:T(8,128)S(1)} fusion(bf16[1,2048,768]{2,1,0:T(8,128)(2,1)S(1)} %copy-done, bf16[32,8,2048]{2,1,0:T(8,128)(2,1)} %all-to-all-done.1), kind=kOutput, calls=%fused_computation | convolution fusion | flops 805306368 | bytes 4980736 | tf_op jit(solution)/shard_map/dot_general | solution.py:64
  84.5 2.1 %fusion.9 = f32[32,2,4,2048]{3,0,2,1:T(8,128)S(1)} fusion(bf16[1,384,2048]{2,1,0:T(8,128)(2,1)} %param.21, bf16[32,2,4,384]{3,2,1,0:T(4,128)(2,1)S(1)} %dot_general.32), kind=kOutput, calls=%fused_computation.11 | convolution fusion | flops 402653184 | bytes 3866624 | tf_op jit(solution)/shard_map/dot_general | solution.py:66
  86.8 2.6 %collective-permute-done = f32[32,4,2048]{2,0,1:T(8,128)S(1)} collective-permute-done((f32[32,4,2048]{2,0,1:T(8,128)S(1)}, f32[32,4,2048]{2,0,1:T(8,128)S(1)}, u32[]{:S(2)}, u32[]{:S(2)}) %collective-permute-start) | collective-permute-done | bytes 1048608 | tf_op jit(solution)/shard_map/ppermute | solution.py:21
  89.6 1.2 %copy.36 = bf16[32,4,2048]{2,1,0:T(4,128)(2,1)} copy(bf16[32,4,2048]{2,0,1:T(8,128)(2,1)S(1)} %fusion.23) | data formatting | bytes 1048576 | tf_op jit(solution)/shard_map/convert_element_type | solution.py:128
  90.8 3.8 %all-to-all-start.2 = ((bf16[32,4,2048]{2,1,0:T(4,128)(2,1)}), bf16[32,4,2048]{2,1,0:T(4,128)(2,1)}, u32[]{:S(2)}, u32[]{:S(2)}) async-start(bf16[32,4,2048]{2,1,0:T(4,128)(2,1)} %copy.36), calls=%async_computation.3 | async-start | bytes 1048576 | tf_op jit(solution)/shard_map/all_to_all | solution.py:129
  94.9 15.2 %all-to-all-done.2 = bf16[32,4,2048]{2,1,0:T(4,128)(2,1)} async-done(((bf16[32,4,2048]{2,1,0:T(4,128)(2,1)}), bf16[32,4,2048]{2,1,0:T(4,128)(2,1)}, u32[]{:S(2)}, u32[]{:S(2)}) %all-to-all-start.2) | async-done | bytes 524320 | tf_op jit(solution)/shard_map/all_to_all | solution.py:129
  110.1 2.0 %reshape_reshape.4 = bf16[128,2048]{1,0:T(8,128)(2,1)} reshape(bf16[32,4,2048]{2,1,0:T(4,128)(2,1)} %all-to-all-done.2) | data formatting | bytes 1048576 | tf_op jit(solution)/shard_map/reshape;reshape | solution.py:133
  112.1 2.0 %convolution_convert_fusion.1 = bf16[8,2048]{1,0:T(8,128)(2,1)} fusion(f32[128,8]{0,1:T(8,128)S(1)} %select_reduce_fusion, bf16[128,2048]{1,0:T(8,128)(2,1)} %reshape_reshape.4), kind=kOutput, calls=%fused_computation.4 | convolution fusion | flops 25182208 | bytes 561152 | tf_op jit(solution)/shard_map/dot_general | solution.py:131
  (35 shorter events, 1.7 us)
Async XLA Ops:
  7.2 74.9 %copy-start = (bf16[1,2048,768]{2,1,0:T(8,128)(2,1)S(1)}, bf16[1,2048,768]{2,1,0:T(8,128)(2,1)}, u32[]{:S(2)}) copy-start(bf16[1,2048,768]{2,1,0:T(8,128)(2,1)} %param.20) | copy-start | bytes 9437188
  8.9 2.5 %copy-start.2 = (bf16[8,4096]{1,0:T(8,128)(2,1)S(1)}, bf16[8,4096]{1,0:T(8,128)(2,1)}, u32[]{:S(2)}) copy-start(bf16[8,4096]{1,0:T(8,128)(2,1)} %param.11) | copy-start | bytes 196612
  12.8 5.5 %copy-start.3 = (s32[8,8]{1,0:T(8,128)S(1)}, s32[8,8]{1,0:T(8,128)}, u32[]{:S(2)}) copy-start(s32[8,8]{1,0:T(8,128)} %param.18) | copy-start | bytes 772
  14.0 8.3 %all-to-all-start = ((bf16[8,4,1024]{2,0,1:T(8,128)(2,1)}), bf16[8,4,1024]{2,0,1:T(8,128)(2,1)S(1)}, u32[]{:S(2)}, u32[]{:S(2)}) async-start(bf16[8,4,1024]{2,0,1:T(8,128)(2,1)} %copy.34), calls=%async_computation | async-start | bytes 131072 | tf_op jit(solution)/shard_map/all_to_all | solution.py:87
  18.3 28.9 %reduce-scatter.2.cloned.1.call-start = ((), (), s32[]{:S(2)}) async-start(), calls=%async_computation.4 | async-start | bytes 327680 | tf_op jit(solution)/shard_map/reduce_scatter | solution.py:88
  18.3 28.8 %copy-start.1 = (bf16[8,2048]{1,0:T(8,128)(2,1)S(1)}, bf16[8,2048]{1,0:T(8,128)(2,1)}, u32[]{:S(2)}) copy-start(bf16[8,2048]{1,0:T(8,128)(2,1)} %param.15) | copy-start | bytes 98308
  18.3 30.4 %copy-start.5 = (f32[2048]{0:T(1024)S(1)}, f32[2048]{0:T(1024)}, u32[]{:S(2)}) copy-start(f32[2048]{0:T(1024)} %param.17) | copy-start | bytes 24580
  51.1 31.0 %all-to-all-start.1 = ((bf16[32,8,2048]{2,1,0:T(8,128)(2,1)}), bf16[32,8,2048]{2,1,0:T(8,128)(2,1)}, u32[]{:S(2)}, u32[]{:S(2)}) async-start(bf16[32,8,2048]{2,1,0:T(8,128)(2,1)} %bitcast.63), calls=%async_computation.2 | async-start | bytes 2097152 | tf_op jit(solution)/shard_map/all_to_all | solution.py:120
  86.7 2.7 %collective-permute-start = (f32[32,4,2048]{2,0,1:T(8,128)S(1)}, f32[32,4,2048]{2,0,1:T(8,128)S(1)}, u32[]{:S(2)}, u32[]{:S(2)}) collective-permute-start(f32[32,4,2048]{2,0,1:T(8,128)S(1)} %select_bitcast_fusion), channel_id=1, source_target_pairs={{0,1},{1,0},{2,3},{3,2},{4,5},{5,4},{6,7},{7,6},{8,9},{9,8},{10,11... | collective-permute-start | bytes 3145736 | tf_op jit(solution)/shard_map/ppermute | solution.py:21
  89.6 5.0 %copy-start.4 = (s32[8,8]{1,0:T(8,128)S(1)}, s32[8,8]{1,0:T(8,128)}, u32[]{:S(2)}) copy-start(s32[8,8]{1,0:T(8,128)} %param.19) | copy-start | bytes 772
  90.8 19.3 %all-to-all-start.2 = ((bf16[32,4,2048]{2,1,0:T(4,128)(2,1)}), bf16[32,4,2048]{2,1,0:T(4,128)(2,1)}, u32[]{:S(2)}, u32[]{:S(2)}) async-start(bf16[32,4,2048]{2,1,0:T(4,128)(2,1)} %copy.36), calls=%async_computation.3 | async-start | bytes 1048576 | tf_op jit(solution)/shard_map/all_to_all | solution.py:129
Sparse Core Ops, SparseCore 0:
  26.2 20.8 reduce-scatter.1
where the time goes:
time: 122 us; the launch traced here: 121 us
  waiting for transfers between devices  68.6 us (56%)
  between operations  14.2 us (12%)
  matrix products  12.9 us (11%)
  starting transfers between devices  12.8 us (10%)
  local copies, waits for them, and re-layouts  7.73 us (6%)
  other arithmetic  4.69 us (4%)
    all_to_all x1, waiting for transfers between devices, body(): lax.all_to_all(doubled, ('dev', 'side'), split_axis=0, concat_axis=0, til...  26.2 us
    reduce_scatter x1, waiting for transfers between devices, body(): lax.psum_scatter(jnp.dot(columns, w_out, preferred_element_type=jnp.float...  20.5 us
    all_to_all x1, waiting for transfers between devices, body(): lax.all_to_all(joined, ('dev', 'side'), split_axis=0, concat_axis=0, tile...  15.2 us
    all_to_all x1, starting transfers between devices, body(): lax.all_to_all(doubled, ('dev', 'side'), split_axis=0, concat_axis=0, til...  4.74 us
    all_to_all x1, starting transfers between devices, body(): lax.all_to_all(attended, 'side', split_axis=1, concat_axis=0, tiled=True)  4.21 us
    all_to_all x1, waiting for transfers between devices, body(): lax.all_to_all(attended, 'side', split_axis=1, concat_axis=0, tiled=True)  4.03 us
    all_to_all x1, starting transfers between devices, body(): lax.all_to_all(joined, ('dev', 'side'), split_axis=0, concat_axis=0, tile...  3.75 us
    dot_general x1, matrix products, body(): jnp.dot(columns, w_out, preferred_element_type=jnp.float32)  3.71 us
  transfers between devices with their start and end apart: 5, of which 5 were waited for; matrix products, arithmetic and copies ran while one was open for 1% of the time, Pallas kernels for 0%

commit v1 on v0

v1 whole, which is shorter than its diff:
```python
import functools
import math

import jax
import jax.numpy as jnp
from jax import lax
from jax.experimental import pallas as pl
from jax.experimental.pallas import tpu as pltpu
from jax.sharding import PartitionSpec as P

HD = 128
LANES = 128
MESH = pl.DeviceIdType.MESH
F32 = jnp.float32
BF16 = jnp.bfloat16


def kernel(
    devs,
    sides,
    lengths_ref,
    queries_ref,
    new_kv_ref,
    residual_ref,
    gain_ref,
    ids_ref,
    level_ref,
    kv_hbm,
    w_out_hbm,
    w_in_hbm,
    w_down_hbm,
    stream_ref,
    sum_ref,
    kv,
    w_out,
    w_in,
    w_down,
    by_head,
    mixed_out,
    mixed_in,
    part_out,
    part_in,
    part_own,
    gathered,
    hidden,
    half_out,
    half_in,
    half_own,
    pair_out,
    pair_in,
    last_out,
    last_in,
    kv_sem,
    weight_sem,
    mixed_send,
    mixed_recv,
    part_send,
    part_recv,
    dev_send,
    dev_recv,
    across_send,
    across_recv,
    sib_send,
    sib_recv,
    half_send,
    half_recv,
    pair_send,
    pair_recv,
    last_send,
    last_recv,
):
    rows, width = residual_ref.shape
    cache = kv_hbm.shape[1]
    heads = queries_ref.shape[1] // HD
    split = new_kv_ref.shape[1] // 2
    kv_heads = split // HD
    group = heads // kv_heads
    side_heads = heads // sides
    pairs = sides // 2
    units = w_down_hbm.shape[1]
    me_d = lax.axis_index("dev")
    me_s = lax.axis_index("side")
    me_p, me_c = me_s // 2, me_s % 2
    sib_s = 2 * me_p + 1 - me_c
    sent = []

    def send(src, dst, send_sem, recv_sem, dev, side):
        copy = pltpu.make_async_remote_copy(
            src_ref=src,
            dst_ref=dst,
            send_sem=send_sem,
            recv_sem=recv_sem,
            device_id={"dev": dev, "side": side},
            device_id_type=MESH,
        )
        copy.start()
        sent.append(copy)

    def arrive(dst, send_sem, recv_sem):
        pltpu.make_async_remote_copy(
            src_ref=dst,
            dst_ref=dst,
            send_sem=send_sem,
            recv_sem=recv_sem,
            device_id={"dev": me_d, "side": sib_s},
            device_id_type=MESH,
        ).wait_recv()

    barrier = pltpu.get_barrier_semaphore()
    for k in range(1, sides):
        pl.semaphore_signal(
            barrier, inc=1, device_id={"side": (me_s + k) % sides}, device_id_type=MESH
        )
    for k in range(1, devs):
        pl.semaphore_signal(
            barrier, inc=1, device_id={"dev": (me_d + k) % devs}, device_id_type=MESH
        )

    kv_copies = []
    for r in range(rows):
        kv_copies.append(pltpu.make_async_copy(kv_hbm.at[r], kv.at[r], kv_sem.at[r]))
        kv_copies[-1].start()
    out_copy = pltpu.make_async_copy(w_out_hbm, w_out, weight_sem.at[0])
    in_copy = pltpu.make_async_copy(w_in_hbm.at[0], w_in, weight_sem.at[1])
    down_copy = pltpu.make_async_copy(w_down_hbm.at[0], w_down, weight_sem.at[2])
    out_copy.start()
    in_copy.start()
    down_copy.start()

    for h in range(heads):
        by_head[pl.ds(h, rows, stride=heads), :] = queries_ref[:, h * HD : (h + 1) * HD].astype(F32)
    new_key = new_kv_ref[:, :split].astype(F32)
    new_value = new_kv_ref[:, split:].astype(F32)
    scaling = 1.0 / math.sqrt(HD)
    head_group = lax.broadcasted_iota(jnp.int32, (heads, split), 0) // group
    lane_group = lax.broadcasted_iota(jnp.int32, (heads, split), 1) // HD
    own_lanes = head_group == lane_group
    position = lax.broadcasted_iota(jnp.int32, (heads, cache), 1)
    for r in range(rows):
        kv_copies[r].wait()
        query = by_head[r * heads : (r + 1) * heads, :]
        wide = jnp.where(own_lanes, jnp.concatenate([query] * kv_heads, axis=1), 0.0)
        scores = (
            lax.dot_general(
                wide.astype(BF16),
                kv[r, :, :split],
                (((1,), (1,)), ((), ())),
                preferred_element_type=F32,
            )
            * scaling
        )
        own_score = jnp.sum(wide * new_key[r : r + 1, :], axis=1, keepdims=True) * scaling
        visible = position < lengths_ref[r]
        scores = jnp.where(visible, scores, -jnp.inf)
        peak = jnp.maximum(jnp.max(scores, axis=1, keepdims=True), own_score)
        weights = jnp.exp(scores - peak)
        own_weight = jnp.exp(own_score - peak)
        denominator = jnp.sum(weights, axis=1, keepdims=True) + own_weight
        probability = (weights / denominator).astype(BF16)
        own_prob = (own_weight / denominator).astype(BF16).astype(F32)
        mixed = jnp.dot(probability, kv[r, :, split:], preferred_element_type=F32)
        mixed = jnp.where(own_lanes, mixed + own_prob * new_value[r : r + 1, :], 0.0)
        narrow = mixed[:, :HD]
        for g in range(1, kv_heads):
            narrow = narrow + mixed[:, g * HD : (g + 1) * HD]
        by_head[r * heads : (r + 1) * heads, :] = narrow
    for s in range(sides):
        taken = [
            by_head[pl.ds(s * side_heads + h, rows, stride=heads), :] for h in range(side_heads)
        ]
        mixed_out[s] = jnp.concatenate(taken, axis=1).astype(BF16)

    pl.semaphore_wait(barrier, sides - 1 + devs - 1)
    for k in range(1, sides):
        to = (me_s + k) % sides
        send(
            mixed_out.at[to], mixed_in.at[me_s], mixed_send.at[k - 1], mixed_recv.at[k - 1], me_d, to
        )
    mixed_in[me_s] = mixed_out[me_s]
    ids = ids_ref[...]
    levels = level_ref[...].astype(F32)
    expert_lane = lax.broadcasted_iota(jnp.int32, (rows, LANES), 1)
    spread = jnp.zeros((rows, LANES), F32)
    for k in range(ids.shape[1]):
        spread = spread + jnp.where(ids[:, k : k + 1] == expert_lane, levels[:, k : k + 1], 0.0)
    gathered[me_p, me_d, me_c, :, width:] = spread.astype(BF16)
    out_copy.wait()
    for k in range(1, sides):
        arrive(mixed_in.at[(me_s + sides - k) % sides], mixed_send.at[k - 1], mixed_recv.at[k - 1])
    features = jnp.concatenate([mixed_in[s].astype(F32) for s in range(sides)], axis=0)
    part = jnp.dot(features.astype(BF16), w_out[...], preferred_element_type=F32)
    part = part.reshape(sides, rows, width)
    part_own[...] = part
    part_out[...] = part.astype(BF16)
    for k in range(1, sides):
        to = (me_s + k) % sides
        send(part_out.at[to], part_in.at[k - 1], part_send.at[k - 1], part_recv.at[k - 1], me_d, to)
    stream = residual_ref[...].astype(F32) + part_own[me_s]
    for k in range(1, sides):
        arrive(part_in.at[k - 1], part_send.at[k - 1], part_recv.at[k - 1])
        stream = stream + part_in[k - 1].astype(F32)
    mean_square = jnp.mean(stream * stream, axis=1, keepdims=True)
    normed = stream * lax.rsqrt(mean_square + 1e-06) * gain_ref[...]
    gathered[me_p, me_d, me_c, :, :width] = normed.astype(BF16)

    def share(j, k, block):
        send(block, block, sib_send.at[j, k], sib_recv.at[j, k], me_d, sib_s)

    def across(k, block):
        for j in range(1, pairs):
            to = 2 * ((me_p + j) % pairs) + me_c
            send(block, block, across_send.at[j - 1, k], across_recv.at[j - 1, k], me_d, to)

    mine = gathered.at[me_p, me_d, me_c]
    for k in range(1, devs):
        send(mine, mine, dev_send.at[k - 1], dev_recv.at[k - 1], (me_d + k) % devs, me_s)
    across(0, mine)
    share(0, 0, mine)
    stream_ref[...] = stream.astype(BF16)
    for k in range(1, devs):
        block = gathered.at[me_p, (me_d + devs - k) % devs, me_c]
        arrive(block, dev_send.at[k - 1], dev_recv.at[k - 1])
        across(k, block)
        share(0, k, block)

    def from_sibling(j):
        for k in range(devs):
            block = gathered.at[(me_p + pairs - j) % pairs, (me_d + devs - k) % devs, 1 - me_c]
            arrive(block, sib_send.at[j, k], sib_recv.at[j, k])

    tokens = devs * 2 * rows
    expert = me_d * pairs + me_p
    token_lane = lax.broadcasted_iota(jnp.int32, (tokens, LANES), 1)

    def first_half(j):
        block = gathered[(me_p + pairs - j) % pairs].astype(F32).reshape(tokens, width + LANES)
        gate_up = jnp.dot(block[:, :width].astype(BF16), w_in[...], preferred_element_type=F32)
        gate = gate_up[:, :units]
        hidden[j] = (gate / (1.0 + jnp.exp(-gate)) * gate_up[:, units:]).astype(BF16)

    def second_half(j):
        level = gathered[(me_p + pairs - j) % pairs, :, :, :, width:].astype(F32)
        level = level.reshape(tokens, LANES)
        chosen = jnp.sum(jnp.where(token_lane == expert, level, 0.0), axis=1, keepdims=True)
        weight = chosen / jnp.sum(level, axis=1, keepdims=True)
        out = jnp.dot(hidden[j], w_down[...], preferred_element_type=F32) * weight
        out = out.reshape(devs, 2, rows, width)
        half_own[j] = jnp.where(me_c == 0, out[:, 0], out[:, 1])
        half_out[j] = jnp.where(me_c == 0, out[:, 1], out[:, 0]).astype(BF16)
        send(half_out.at[j], half_in.at[j], half_send.at[j], half_recv.at[j], me_d, sib_s)

    in_copy.wait()
    from_sibling(0)
    first_half(0)
    for j in range(1, pairs):
        for k in range(devs):
            block = gathered.at[(me_p + pairs - j) % pairs, (me_d + devs - k) % devs, me_c]
            arrive(block, across_send.at[j - 1, k], across_recv.at[j - 1, k])
            share(j, k, block)
    down_copy.wait()
    for j in range(1, pairs):
        from_sibling(j)
        first_half(j)
        second_half(j)
    second_half(0)

    for j in range(1, pairs):
        arrive(half_in.at[j], half_send.at[j], half_recv.at[j])
        to = 2 * ((me_p + pairs - j) % pairs) + me_c
        for k in range(1, devs + 1):
            dev = (me_d + k) % devs
            pair_out[j - 1, dev] = (half_own[j, dev] + half_in[j, dev].astype(F32)).astype(BF16)
            send(
                pair_out.at[j - 1, dev],
                pair_in.at[j - 1, dev],
                pair_send.at[j - 1, k - 1],
                pair_recv.at[j - 1, k - 1],
                me_d,
                to,
            )
    arrive(half_in.at[0], half_send.at[0], half_recv.at[0])
    total = None
    for k in range(1, devs + 1):
        dev = (me_d + k) % devs
        total = half_own[0, dev] + half_in[0, dev].astype(F32)
        for j in range(1, pairs):
            arrive(pair_in.at[j - 1, dev], pair_send.at[j - 1, k - 1], pair_recv.at[j - 1, k - 1])
            total = total + pair_in[j - 1, dev].astype(F32)
        if k < devs:
            last_out[k - 1] = total.astype(BF16)
            send(
                last_out.at[k - 1],
                last_in.at[k - 1],
                last_send.at[k - 1],
                last_recv.at[k - 1],
                dev,
                me_s,
            )
    for k in range(1, devs):
        arrive(last_in.at[k - 1], last_send.at[k - 1], last_recv.at[k - 1])
        total = total + last_in[k - 1].astype(F32)
    sum_ref[...] = total.astype(BF16)
    for copy in sent:
        copy.wait_send()


def body(
    queries,
    kv_cache,
    new_kv,
    lengths,
    residual,
    w_out,
    norm_gain,
    expert_ids,
    route_level,
    w_in,
    w_down,
):
    devs, sides = lax.axis_size("dev"), lax.axis_size("side")
    pairs = sides // 2
    rows, width = residual.shape
    heads = queries.shape[1] // HD
    units = w_down.shape[1]
    tokens = devs * 2 * rows
    dma = pltpu.SemaphoreType.DMA
    vmem = pl.BlockSpec(memory_space=pltpu.VMEM)
    hbm = pl.BlockSpec(memory_space=pl.ANY)
    return pl.pallas_call(
        functools.partial(kernel, devs, sides),
        out_shape=(
            jax.ShapeDtypeStruct((rows, width), BF16),
            jax.ShapeDtypeStruct((rows, width), BF16),
        ),
        in_specs=[pl.BlockSpec(memory_space=pltpu.SMEM)] + [vmem] * 6 + [hbm] * 4,
        out_specs=(vmem, vmem),
        scratch_shapes=[
            pltpu.VMEM(kv_cache.shape, BF16),
            pltpu.VMEM(w_out.shape, BF16),
            pltpu.VMEM(w_in.shape[1:], BF16),
            pltpu.VMEM(w_down.shape[1:], BF16),
            pltpu.VMEM((rows * heads, HD), F32),
            pltpu.VMEM((sides, rows, w_out.shape[0]), BF16),
            pltpu.VMEM((sides, rows, w_out.shape[0]), BF16),
            pltpu.VMEM((sides, rows, width), BF16),
            pltpu.VMEM((sides - 1, rows, width), BF16),
            pltpu.VMEM((sides, rows, width), F32),
            pltpu.VMEM((pairs, devs, 2, rows, width + LANES), BF16),
            pltpu.VMEM((pairs, tokens, units), BF16),
            pltpu.VMEM((pairs, devs, rows, width), BF16),
            pltpu.VMEM((pairs, devs, rows, width), BF16),
            pltpu.VMEM((pairs, devs, rows, width), F32),
            pltpu.VMEM((max(1, pairs - 1), devs, rows, width), BF16),
            pltpu.VMEM((max(1, pairs - 1), devs, rows, width), BF16),
            pltpu.VMEM((devs - 1, rows, width), BF16),
            pltpu.VMEM((devs - 1, rows, width), BF16),
            dma((rows,)),
            dma((3,)),
            dma((sides - 1,)),
            dma((sides - 1,)),
            dma((sides - 1,)),
            dma((sides - 1,)),
            dma((devs - 1,)),
            dma((devs - 1,)),
            dma((max(1, pairs - 1), devs)),
            dma((max(1, pairs - 1), devs)),
            dma((pairs, devs)),
            dma((pairs, devs)),
            dma((pairs,)),
            dma((pairs,)),
            dma((max(1, pairs - 1), devs)),
            dma((max(1, pairs - 1), devs)),
            dma((devs - 1,)),
            dma((devs - 1,)),
        ],
        compiler_params=pltpu.CompilerParams(
            collective_id=0, has_side_effects=True, vmem_limit_bytes=56 * 1024 * 1024
        ),
    )(
        lengths,
        queries,
        new_kv,
        residual,
        norm_gain.reshape(1, -1),
        expert_ids,
        route_level,
        kv_cache,
        w_out,
        w_in,
        w_down,
    )


def solution(mesh):
    return jax.shard_map(
        body,
        mesh=mesh,
        in_specs=(
            P(("groups", "dev", "side"), None),
            P(("groups", "dev", "side"), None, None),
            P(("groups", "dev", "side"), None),
            P(("groups", "dev", "side")),
            P(("groups", "dev", "side"), None),
            P("side", None),
            P(),
            P(("groups", "dev", "side"), None),
            P(("groups", "dev", "side"), None),
            P(("dev", "side"), None, None),
            P(("dev", "side"), None, None),
        ),
        out_specs=(P(("groups", "dev", "side"), None), P(("groups", "dev", "side"), None)),
        check_vma=False,
    )
```

time: 122 us -> 46.3 us (0.38)
  waiting for transfers between devices: 68.6 us -> 0 us
  Pallas kernels: 0 us -> 42.6 us
  between operations: 14.2 us -> 0.64 us
  matrix products: 12.9 us -> 0 us
  starting transfers between devices: 12.8 us -> 0 us
  local copies, waits for them, and re-layouts: 7.73 us -> 2.75 us
  other arithmetic: 4.69 us -> 0 us
    all_to_all x3 -> x0, waiting for transfers between devices: 45.5 us -> none  [the longest x1 26.2 us: body(): lax.all_to_all(doubled, ('dev', 'side'), split_axis=0, concat_axis=0, til...]
    pallas_call x0 -> x1, Pallas kernels: none -> 42.6 us  [body(): pl.pallas_call(functools.partial(kernel, devs, sides), out_shape=(jax.Sha...]
    reduce_scatter x1 -> x0, waiting for transfers between devices: 20.5 us -> none  [body(): lax.psum_scatter(jnp.dot(columns, w_out, preferred_element_type=jnp.float...]
    dot_general x8 -> x0, matrix products: 12.9 us -> none  [the longest x1 3.71 us: body(): jnp.dot(columns, w_out, preferred_element_type=jnp.float32)]
    all_to_all x3 -> x0, starting transfers between devices: 12.7 us -> none  [the longest x1 4.74 us: body(): lax.all_to_all(doubled, ('dev', 'side'), split_axis=0, concat_axis=0, til...]
    ppermute x1 -> x0, waiting for transfers between devices: 2.65 us -> none  [partner(): return lax.ppermute(block, axis, route)]
    reduce_sum x5 -> x0, other arithmetic: 2.19 us -> none  [the longest x1 1.57 us: body(): mean_square = jnp.mean(stream * stream, axis=1, keepdims=True)]
    another operation x1 -> x0, local copies, waits for them, and re-layouts: 1.97 us -> none  [body(): outputs.reshape(experts * capacity, model_width).astype(jnp.float32)]
  transfers between devices with their start and end apart: 5 -> 0, of which waited for: 5 -> 0; matrix products, arithmetic and copies ran while one was open for 1% -> 0% of each run, Pallas kernels for 0% -> 0%
where the time goes in v1:
time: 46.3 us; the launch traced here: 46 us
  Pallas kernels  42.6 us (92%)
  local copies, waits for them, and re-layouts  2.75 us (6%)
  between operations  0.64 us (1%)
    pallas_call x1, Pallas kernels, body(): pl.pallas_call(functools.partial(kernel, devs, sides), out_shape=(jax.Sha...  42.6 us
    unnamed x2, local copies, waits for them, and re-layouts  2.75 us

profile of v1, /device:TPU:0, one launch (start us, length us, event | category | flops | bytes accessed | tf_op | source)
XLA Modules:
  0.0 46.0 jit_solution(11187266724792225510)
XLA Ops:
  0.6 42.6 %shard_map.122 = (bf16[8,2048]{1,0:T(8,128)(2,1)}, bf16[8,2048]{1,0:T(8,128)(2,1)}) custom-call(s32[8]{0:T(128)} %lengths_ref.1, bf16[8,4096]{1,0:T(8,128)(2,1)} %queries_ref.1, bf16[8,1024]{1,0:T(8,128)(2,1)} %new_kv_ref.1, bf16[8,2048]{1,0:T(8,128)(2,1)} %residual_ref.1, f32[1,2048]{1,0:T(1,128)} %bitcast.1, s32[8,8]{1,0:T(8,128)} %ids_ref.1, ...), custom_call_target="tpu_custom_call" | custom-call | tf_op jit(solution)/shard_map/pallas_call | solution.py:329
  43.2 1.4 %copy.15 = bf16[8,2048]{1,0:T(8,128)(2,1)} copy(bf16[8,2048]{1,0:T(8,128)(2,1)} %get-tuple-element.4) | data formatting | bytes 65536
  44.6 1.4 %copy.16 = bf16[8,2048]{1,0:T(8,128)(2,1)} copy(bf16[8,2048]{1,0:T(8,128)(2,1)} %get-tuple-element.5) | data formatting | bytes 65536

commit v2 on v1

--- a/solution.py
+++ b/solution.py
@@ -19,18 +19,24 @@
     devs,
     sides,
     lengths_ref,
+    queries_hbm,
+    new_kv_hbm,
+    residual_hbm,
+    gain_hbm,
+    ids_hbm,
+    level_hbm,
+    kv_hbm,
+    w_out_hbm,
+    w_in_hbm,
+    w_down_hbm,
+    stream_ref,
+    sum_ref,
     queries_ref,
     new_kv_ref,
     residual_ref,
     gain_ref,
     ids_ref,
     level_ref,
-    kv_hbm,
-    w_out_hbm,
-    w_in_hbm,
-    w_down_hbm,
-    stream_ref,
-    sum_ref,
     kv,
     w_out,
     w_in,
@@ -50,6 +56,7 @@
     pair_in,
     last_out,
     last_in,
+    small_sem,
     kv_sem,
     weight_sem,
     mixed_send,
@@ -106,20 +113,20 @@
             device_id_type=MESH,
         ).wait_recv()
 
-    barrier = pltpu.get_barrier_semaphore()
-    for k in range(1, sides):
-        pl.semaphore_signal(
-            barrier, inc=1, device_id={"side": (me_s + k) % sides}, device_id_type=MESH
-        )
-    for k in range(1, devs):
-        pl.semaphore_signal(
-            barrier, inc=1, device_id={"dev": (me_d + k) % devs}, device_id_type=MESH
-        )
-
-    kv_copies = []
-    for r in range(rows):
-        kv_copies.append(pltpu.make_async_copy(kv_hbm.at[r], kv.at[r], kv_sem.at[r]))
-        kv_copies[-1].start()
+    small = (
+        (queries_hbm, queries_ref),
+        (new_kv_hbm, new_kv_ref),
+        (residual_hbm, residual_ref),
+        (gain_hbm, gain_ref),
+        (ids_hbm, ids_ref),
+        (level_hbm, level_ref),
+    )
+    small_copies = [
+        pltpu.make_async_copy(src, dst, small_sem.at[i]) for i, (src, dst) in enumerate(small)
+    ]
+    kv_copies = [pltpu.make_async_copy(kv_hbm.at[r], kv.at[r], kv_sem.at[r]) for r in range(rows)]
+    for copy in small_copies[:2] + kv_copies + small_copies[2:]:
+        copy.start()
     out_copy = pltpu.make_async_copy(w_out_hbm, w_out, weight_sem.at[0])
     in_copy = pltpu.make_async_copy(w_in_hbm.at[0], w_in, weight_sem.at[1])
     down_copy = pltpu.make_async_copy(w_down_hbm.at[0], w_down, weight_sem.at[2])
@@ -127,6 +134,18 @@
     in_copy.start()
     down_copy.start()
 
+    barrier = pltpu.get_barrier_semaphore()
+    for k in range(1, sides):
+        pl.semaphore_signal(
+            barrier, inc=1, device_id={"side": (me_s + k) % sides}, device_id_type=MESH
+        )
+    for k in range(1, devs):
+        pl.semaphore_signal(
+            barrier, inc=1, device_id={"dev": (me_d + k) % devs}, device_id_type=MESH
+        )
+
+    small_copies[0].wait()
+    small_copies[1].wait()
     for h in range(heads):
         by_head[pl.ds(h, rows, stride=heads), :] = queries_ref[:, h * HD : (h + 1) * HD].astype(F32)
     new_key = new_kv_ref[:, :split].astype(F32)
@@ -136,33 +155,50 @@
     lane_group = lax.broadcasted_iota(jnp.int32, (heads, split), 1) // HD
     own_lanes = head_group == lane_group
     position = lax.broadcasted_iota(jnp.int32, (heads, cache), 1)
+    wide = [
+        jnp.where(
+            own_lanes,
+            jnp.concatenate([by_head[r * heads : (r + 1) * heads, :]] * kv_heads, axis=1),
+            0.0,
+        )
+        for r in range(rows)
+    ]
+    own_score = [
+        jnp.sum(wide[r] * new_key[r : r + 1, :], axis=1, keepdims=True) * scaling
+        for r in range(rows)
+    ]
+    for copy in kv_copies:
+        copy.wait()
+    scores = [
+        lax.dot_general(
+            wide[r].astype(BF16),
+            kv[r, :, :split],
+            (((1,), (1,)), ((), ())),
+            preferred_element_type=F32,
+        )
+        for r in range(rows)
+    ]
+    scores = [
+        jnp.where(position < lengths_ref[r], scores[r] * scaling, -jnp.inf) for r in range(rows)
+    ]
+    peak = [
+        jnp.maximum(jnp.max(scores[r], axis=1, keepdims=True), own_score[r]) for r in range(rows)
+    ]
+    weights = [jnp.exp(scores[r] - peak[r]) for r in range(rows)]
+    own_weight = [jnp.exp(own_score[r] - peak[r]) for r in range(rows)]
+    denominator = [
+        jnp.sum(weights[r], axis=1, keepdims=True) + own_weight[r] for r in range(rows)
+    ]
+    probability = [(weights[r] / denominator[r]).astype(BF16) for r in range(rows)]
+    own_prob = [(own_weight[r] / denominator[r]).astype(BF16).astype(F32) for r in range(rows)]
+    mixed = [
+        jnp.dot(probability[r], kv[r, :, split:], preferred_element_type=F32) for r in range(rows)
+    ]
     for r in range(rows):
-        kv_copies[r].wait()
-        query = by_head[r * heads : (r + 1) * heads, :]
-        wide = jnp.where(own_lanes, jnp.concatenate([query] * kv_heads, axis=1), 0.0)
-        scores = (
-            lax.dot_general(
-                wide.astype(BF16),
-                kv[r, :, :split],
-                (((1,), (1,)), ((), ())),
-                preferred_element_type=F32,
-            )
-            * scaling
-        )
-        own_score = jnp.sum(wide * new_key[r : r + 1, :], axis=1, keepdims=True) * scaling
-        visible = position < lengths_ref[r]
-        scores = jnp.where(visible, scores, -jnp.inf)
-        peak = jnp.maximum(jnp.max(scores, axis=1, keepdims=True), own_score)
-        weights = jnp.exp(scores - peak)
-        own_weight = jnp.exp(own_score - peak)
-        denominator = jnp.sum(weights, axis=1, keepdims=True) + own_weight
-        probability = (weights / denominator).astype(BF16)
-        own_prob = (own_weight / denominator).astype(BF16).astype(F32)
-        mixed = jnp.dot(probability, kv[r, :, split:], preferred_element_type=F32)
-        mixed = jnp.where(own_lanes, mixed + own_prob * new_value[r : r + 1, :], 0.0)
-        narrow = mixed[:, :HD]
+        whole = jnp.where(own_lanes, mixed[r] + own_prob[r] * new_value[r : r + 1, :], 0.0)
+        narrow = whole[:, :HD]
         for g in range(1, kv_heads):
-            narrow = narrow + mixed[:, g * HD : (g + 1) * HD]
+            narrow = narrow + whole[:, g * HD : (g + 1) * HD]
         by_head[r * heads : (r + 1) * heads, :] = narrow
     for s in range(sides):
         taken = [
@@ -177,6 +213,8 @@
             mixed_out.at[to], mixed_in.at[me_s], mixed_send.at[k - 1], mixed_recv.at[k - 1], me_d, to
         )
     mixed_in[me_s] = mixed_out[me_s]
+    for copy in small_copies[2:]:
+        copy.wait()
     ids = ids_ref[...]
     levels = level_ref[...].astype(F32)
     expert_lane = lax.broadcasted_iota(jnp.int32, (rows, LANES), 1)
@@ -304,6 +342,17 @@
         copy.wait_send()
 
 
+def hand_out(stream_ref, sum_ref, stream_out, sum_out, sem):
+    copies = [
+        pltpu.make_async_copy(stream_ref, stream_out, sem.at[0]),
+        pltpu.make_async_copy(sum_ref, sum_out, sem.at[1]),
+    ]
+    for copy in copies:
+        copy.start()
+    for copy in copies:
+        copy.wait()
+
+
 def body(
     queries,
     kv_cache,
@@ -326,15 +375,18 @@
     dma = pltpu.SemaphoreType.DMA
     vmem = pl.BlockSpec(memory_space=pltpu.VMEM)
     hbm = pl.BlockSpec(memory_space=pl.ANY)
-    return pl.pallas_call(
+    norm_gain = norm_gain.reshape(1, -1)
+    small = (queries, new_kv, residual, norm_gain, expert_ids, route_level)
+    results = pl.pallas_call(
         functools.partial(kernel, devs, sides),
         out_shape=(
             jax.ShapeDtypeStruct((rows, width), BF16),
             jax.ShapeDtypeStruct((rows, width), BF16),
         ),
-        in_specs=[pl.BlockSpec(memory_space=pltpu.SMEM)] + [vmem] * 6 + [hbm] * 4,
+        in_specs=[pl.BlockSpec(memory_space=pltpu.SMEM)] + [hbm] * 10,
         out_specs=(vmem, vmem),
         scratch_shapes=[
+            *(pltpu.VMEM(x.shape, x.dtype) for x in small),
             pltpu.VMEM(kv_cache.shape, BF16),
             pltpu.VMEM(w_out.shape, BF16),
             pltpu.VMEM(w_in.shape[1:], BF16),
@@ -354,6 +406,7 @@
             pltpu.VMEM((max(1, pairs - 1), devs, rows, width), BF16),
             pltpu.VMEM((devs - 1, rows, width), BF16),
             pltpu.VMEM((devs - 1, rows, width), BF16),
+            dma((len(small),)),
             dma((rows,)),
             dma((3,)),
             dma((sides - 1,)),
@@ -378,17 +431,20 @@
         ),
     )(
         lengths,
-        queries,
-        new_kv,
-        residual,
-        norm_gain.reshape(1, -1),
-        expert_ids,
-        route_level,
+        *small,
         kv_cache,
         w_out,
         w_in,
         w_down,
     )
+    return pl.pallas_call(
+        hand_out,
+        out_shape=tuple(jax.ShapeDtypeStruct((rows, width), BF16) for _ in results),
+        in_specs=[hbm] * 2,
+        out_specs=(hbm, hbm),
+        scratch_shapes=[dma((2,))],
+        compiler_params=pltpu.CompilerParams(vmem_limit_bytes=56 * 1024 * 1024),
+    )(*results)
 
 
 def solution(mesh):

time: 46.3 us -> 45.9 us (level)
  local copies, waits for them, and re-layouts: 2.75 us -> 0 us
  Pallas kernels: 42.6 us -> 45.1 us
    pallas_call x0 -> x1, Pallas kernels: none -> 3.11 us  [body(): pl.pallas_call(hand_out, out_shape=tuple((jax.ShapeDtypeStruct((rows, wid...]
    unnamed x2 -> x0, local copies, waits for them, and re-layouts: 2.75 us -> none
    pallas_call x1, Pallas kernels: 42.6 us -> 42 us  [body(): pl.pallas_call(functools.partial(kernel, devs, sides), out_shape=(jax.Sha...]
where the time goes in v2:
time: 45.9 us; the launch traced here: 45.8 us
  Pallas kernels  45.1 us (98%)
  between operations  0.64 us (1%)
    pallas_call x1, Pallas kernels, body(): pl.pallas_call(functools.partial(kernel, devs, sides), out_shape=(jax.Sha...  42 us
    pallas_call x1, Pallas kernels, body(): pl.pallas_call(hand_out, out_shape=tuple((jax.ShapeDtypeStruct((rows, wid...  3.11 us

profile of v2, /device:TPU:0, one launch (start us, length us, event | category | flops | bytes accessed | tf_op | source)
XLA Modules:
  0.0 45.8 jit_solution(11040404012802851756)
XLA Ops:
  0.6 42.0 %shard_map.122 = (bf16[8,2048]{1,0:T(8,128)(2,1)}, bf16[8,2048]{1,0:T(8,128)(2,1)}) custom-call(s32[8]{0:T(128)} %lengths_ref.1, bf16[8,4096]{1,0:T(8,128)(2,1)} %queries_hbm.1, bf16[8,1024]{1,0:T(8,128)(2,1)} %new_kv_hbm.1, bf16[8,2048]{1,0:T(8,128)(2,1)} %residual_hbm.1, f32[1,2048]{1,0:T(1,128)} %bitcast.1, s32[8,8]{1,0:T(8,128)} %ids_hbm.1, ...), custom_call_target="tpu_custom_call" | custom-call | tf_op jit(solution)/shard_map/pallas_call | solution.py:380
  42.7 3.1 %shard_map.123 = (bf16[8,2048]{1,0:T(8,128)(2,1)}, bf16[8,2048]{1,0:T(8,128)(2,1)}) custom-call(bf16[8,2048]{1,0:T(8,128)(2,1)} %get-tuple-element.4.stream_ref, bf16[8,2048]{1,0:T(8,128)(2,1)} %get-tuple-element.5.sum_ref), custom_call_target="tpu_custom_call" | custom-call | tf_op jit(solution)/shard_map/pallas_call | solution.py:440

commit v3 on v2

--- a/solution.py
+++ b/solution.py
@@ -48,14 +48,15 @@
     part_in,
     part_own,
     gathered,
-    hidden,
     half_out,
     half_in,
     half_own,
-    pair_out,
-    pair_in,
-    last_out,
-    last_in,
+    second_out,
+    second_in,
+    first_out,
+    first_in,
+    column_out,
+    column_in,
     small_sem,
     kv_sem,
     weight_sem,
@@ -63,18 +64,22 @@
     mixed_recv,
     part_send,
     part_recv,
-    dev_send,
-    dev_recv,
-    across_send,
-    across_recv,
+    column_send,
+    column_recv,
+    first_send,
+    first_recv,
+    second_send,
+    second_recv,
     sib_send,
     sib_recv,
     half_send,
     half_recv,
-    pair_send,
-    pair_recv,
-    last_send,
-    last_recv,
+    second_back_send,
+    second_back_recv,
+    first_back_send,
+    first_back_recv,
+    column_back_send,
+    column_back_recv,
 ):
     rows, width = residual_ref.shape
     cache = kv_hbm.shape[1]
@@ -89,7 +94,21 @@
     me_s = lax.axis_index("side")
     me_p, me_c = me_s // 2, me_s % 2
     sib_s = 2 * me_p + 1 - me_c
+    near = 2 if devs % 2 == 0 else 1
+    columns = devs // near
+    me_z, me_y = me_d // near, me_d % near
+    flip = me_c if pairs == 2 and near == 2 else 0
     sent = []
+
+    def first_of(p, y):
+        return p + flip * (1 - 2 * p), y + (1 - flip) * (1 - 2 * y)
+
+    def second_of(p, y, j):
+        return (1 - flip) * ((p + j) % pairs) + flip * p, y + flip * (1 - 2 * y)
+
+    def device(p, z, y):
+        return z * near + y, 2 * p + me_c
+
 
     def send(src, dst, send_sem, recv_sem, dev, side):
         copy = pltpu.make_async_remote_copy(
@@ -221,7 +240,7 @@
     spread = jnp.zeros((rows, LANES), F32)
     for k in range(ids.shape[1]):
         spread = spread + jnp.where(ids[:, k : k + 1] == expert_lane, levels[:, k : k + 1], 0.0)
-    gathered[me_p, me_d, me_c, :, width:] = spread.astype(BF16)
+    gathered[me_p, me_z, me_y, me_c, :, width:] = spread.astype(BF16)
     out_copy.wait()
     for k in range(1, sides):
         arrive(mixed_in.at[(me_s + sides - k) % sides], mixed_send.at[k - 1], mixed_recv.at[k - 1])
@@ -239,118 +258,163 @@
         stream = stream + part_in[k - 1].astype(F32)
     mean_square = jnp.mean(stream * stream, axis=1, keepdims=True)
     normed = stream * lax.rsqrt(mean_square + 1e-06) * gain_ref[...]
-    gathered[me_p, me_d, me_c, :, :width] = normed.astype(BF16)
-
-    def share(j, k, block):
-        send(block, block, sib_send.at[j, k], sib_recv.at[j, k], me_d, sib_s)
-
-    def across(k, block):
+    gathered[me_p, me_z, me_y, me_c, :, :width] = normed.astype(BF16)
+
+    def spread_out(k, slot, p, y):
+        block = gathered.at[p, (me_z + columns - k) % columns, y, me_c]
+        if slot == 0:
+            jp, jy = 0, 0
+            if near == 2:
+                dev, side = device(*before(first_of(me_p, me_y)))
+                send(block, block, first_send.at[k], first_recv.at[k], dev, side)
+        else:
+            jp, jy = flip, 1 - flip
         for j in range(1, pairs):
-            to = 2 * ((me_p + j) % pairs) + me_c
-            send(block, block, across_send.at[j - 1, k], across_recv.at[j - 1, k], me_d, to)
-
-    mine = gathered.at[me_p, me_d, me_c]
-    for k in range(1, devs):
-        send(mine, mine, dev_send.at[k - 1], dev_recv.at[k - 1], (me_d + k) % devs, me_s)
-    across(0, mine)
-    share(0, 0, mine)
+            dev, side = device(*before(second_of(me_p, me_y, j)))
+            sems = second_send.at[j - 1, k, slot], second_recv.at[j - 1, k, slot]
+            send(block, block, *sems, dev, side)
+        send(block, block, sib_send.at[jp, k, jy], sib_recv.at[jp, k, jy], me_d, sib_s)
+
+    def before(py):
+        return py[0], me_z, py[1]
+
+    mine = gathered.at[me_p, me_z, me_y, me_c]
+    for k in range(1, columns):
+        dev, side = device(me_p, (me_z + k) % columns, me_y)
+        send(mine, mine, column_send.at[k - 1], column_recv.at[k - 1], dev, side)
+    spread_out(0, 0, me_p, me_y)
     stream_ref[...] = stream.astype(BF16)
-    for k in range(1, devs):
-        block = gathered.at[me_p, (me_d + devs - k) % devs, me_c]
-        arrive(block, dev_send.at[k - 1], dev_recv.at[k - 1])
-        across(k, block)
-        share(0, k, block)
-
-    def from_sibling(j):
-        for k in range(devs):
-            block = gathered.at[(me_p + pairs - j) % pairs, (me_d + devs - k) % devs, 1 - me_c]
-            arrive(block, sib_send.at[j, k], sib_recv.at[j, k])
-
-    tokens = devs * 2 * rows
+    first_p, first_y = first_of(me_p, me_y)
+
+    def take_first(k):
+        if near == 2:
+            block = gathered.at[first_p, (me_z + columns - k) % columns, first_y, me_c]
+            arrive(block, first_send.at[k], first_recv.at[k])
+            spread_out(k, 1, first_p, first_y)
+
+    for k in range(1, columns):
+        block = gathered.at[me_p, (me_z + columns - k) % columns, me_y, me_c]
+        arrive(block, column_send.at[k - 1], column_recv.at[k - 1])
+        spread_out(k, 0, me_p, me_y)
+        take_first(k - 1)
+    take_first(columns - 1)
+    for k in range(columns):
+        for j in range(1, pairs):
+            from_p, from_y = second_of(me_p, me_y, pairs - j)
+            for slot in range(near):
+                if slot == 1:
+                    from_p, from_y = first_of(from_p, from_y)
+                block = gathered.at[from_p, (me_z + columns - k) % columns, from_y, me_c]
+                arrive(block, second_send.at[j - 1, k, slot], second_recv.at[j - 1, k, slot])
+                jp = (1 - flip) * j + flip * slot
+                jy = (1 - flip) * slot + flip
+                send(block, block, sib_send.at[jp, k, jy], sib_recv.at[jp, k, jy], me_d, sib_s)
+    for k in range(columns):
+        for jp in range(pairs):
+            for jy in range(near):
+                block = gathered.at[
+                    (me_p + pairs - jp) % pairs,
+                    (me_z + columns - k) % columns,
+                    (me_y + jy) % near,
+                    1 - me_c,
+                ]
+                arrive(block, sib_send.at[jp, k, jy], sib_recv.at[jp, k, jy])
+
+    in_copy.wait()
+    tokens = pairs * devs * 2 * rows
     expert = me_d * pairs + me_p
     token_lane = lax.broadcasted_iota(jnp.int32, (tokens, LANES), 1)
-
-    def first_half(j):
-        block = gathered[(me_p + pairs - j) % pairs].astype(F32).reshape(tokens, width + LANES)
-        gate_up = jnp.dot(block[:, :width].astype(BF16), w_in[...], preferred_element_type=F32)
-        gate = gate_up[:, :units]
-        hidden[j] = (gate / (1.0 + jnp.exp(-gate)) * gate_up[:, units:]).astype(BF16)
-
-    def second_half(j):
-        level = gathered[(me_p + pairs - j) % pairs, :, :, :, width:].astype(F32)
-        level = level.reshape(tokens, LANES)
-        chosen = jnp.sum(jnp.where(token_lane == expert, level, 0.0), axis=1, keepdims=True)
-        weight = chosen / jnp.sum(level, axis=1, keepdims=True)
-        out = jnp.dot(hidden[j], w_down[...], preferred_element_type=F32) * weight
-        out = out.reshape(devs, 2, rows, width)
-        half_own[j] = jnp.where(me_c == 0, out[:, 0], out[:, 1])
-        half_out[j] = jnp.where(me_c == 0, out[:, 1], out[:, 0]).astype(BF16)
-        send(half_out.at[j], half_in.at[j], half_send.at[j], half_recv.at[j], me_d, sib_s)
-
-    in_copy.wait()
-    from_sibling(0)
-    first_half(0)
-    for j in range(1, pairs):
-        for k in range(devs):
-            block = gathered.at[(me_p + pairs - j) % pairs, (me_d + devs - k) % devs, me_c]
-            arrive(block, across_send.at[j - 1, k], across_recv.at[j - 1, k])
-            share(j, k, block)
+    block = gathered[:, :, :, :, :, :width].astype(F32).reshape(tokens, width).astype(BF16)
+    gate_up = jnp.dot(block, w_in[...], preferred_element_type=F32)
+    gate = gate_up[:, :units]
+    hidden = (gate / (1.0 + jnp.exp(-gate)) * gate_up[:, units:]).astype(BF16)
+    level = gathered[:, :, :, :, :, width:].astype(F32).reshape(tokens, LANES)
+    chosen = jnp.sum(jnp.where(token_lane == expert, level, 0.0), axis=1, keepdims=True)
+    weight = chosen / jnp.sum(level, axis=1, keepdims=True)
     down_copy.wait()
-    for j in range(1, pairs):
-        from_sibling(j)
-        first_half(j)
-        second_half(j)
-    second_half(0)
-
-    for j in range(1, pairs):
-        arrive(half_in.at[j], half_send.at[j], half_recv.at[j])
-        to = 2 * ((me_p + pairs - j) % pairs) + me_c
-        for k in range(1, devs + 1):
-            dev = (me_d + k) % devs
-            pair_out[j - 1, dev] = (half_own[j, dev] + half_in[j, dev].astype(F32)).astype(BF16)
+    half = width // 2
+    for h in range(2):
+        out = jnp.dot(
+            hidden, w_down[:, h * half : (h + 1) * half], preferred_element_type=F32
+        )
+        out = (out * weight).reshape(pairs, columns, near, 2, rows, half)
+        half_own[h] = jnp.where(me_c == 0, out[:, :, :, 0], out[:, :, :, 1])
+        half_out[h] = jnp.where(me_c == 0, out[:, :, :, 1], out[:, :, :, 0]).astype(BF16)
+        send(half_out.at[h], half_in.at[h], half_send.at[h], half_recv.at[h], me_d, sib_s)
+
+    def both(h, p, z, y):
+        return half_own[h, p, z, y] + half_in[h, p, z, y].astype(F32)
+
+    steps = [(h, k % columns) for h in range(2) for k in range(1, columns + 1)]
+    for h, k in steps:
+        if k == 1 % columns:
+            arrive(half_in.at[h], half_send.at[h], half_recv.at[h])
+        z = (me_z + k) % columns
+        for j in range(1, pairs):
+            to_p, to_y = second_of(me_p, me_y, j)
+            dev, side = device(to_p, me_z, to_y)
+            for slot in range(near):
+                if slot == 1:
+                    to_p, to_y = first_of(to_p, to_y)
+                second_out[h, j - 1, k, slot] = both(h, to_p, z, to_y).astype(BF16)
             send(
-                pair_out.at[j - 1, dev],
-                pair_in.at[j - 1, dev],
-                pair_send.at[j - 1, k - 1],
-                pair_recv.at[j - 1, k - 1],
-                me_d,
-                to,
+                second_out.at[h, j - 1, k],
+                second_in.at[h, j - 1, k],
+                second_back_send.at[h, j - 1, k],
+                second_back_recv.at[h, j - 1, k],
+                dev,
+                side,
             )
-    arrive(half_in.at[0], half_send.at[0], half_recv.at[0])
-    total = None
-    for k in range(1, devs + 1):
-        dev = (me_d + k) % devs
-        total = half_own[0, dev] + half_in[0, dev].astype(F32)
+
+    def to_first(h, k):
+        z = (me_z + k) % columns
         for j in range(1, pairs):
-            arrive(pair_in.at[j - 1, dev], pair_send.at[j - 1, k - 1], pair_recv.at[j - 1, k - 1])
-            total = total + pair_in[j - 1, dev].astype(F32)
-        if k < devs:
-            last_out[k - 1] = total.astype(BF16)
-            send(
-                last_out.at[k - 1],
-                last_in.at[k - 1],
-                last_send.at[k - 1],
-                last_recv.at[k - 1],
-                dev,
-                me_s,
+            arrive(
+                second_in.at[h, j - 1, k],
+                second_back_send.at[h, j - 1, k],
+                second_back_recv.at[h, j - 1, k],
             )
-    for k in range(1, devs):
-        arrive(last_in.at[k - 1], last_send.at[k - 1], last_recv.at[k - 1])
-        total = total + last_in[k - 1].astype(F32)
-    sum_ref[...] = total.astype(BF16)
+        if near == 2:
+            total = both(h, first_p, z, first_y)
+            for j in range(1, pairs):
+                total = total + second_in[h, j - 1, k, 1].astype(F32)
+            first_out[h, k] = total.astype(BF16)
+            dev, side = device(first_p, me_z, first_y)
+            sems = first_back_send.at[h, k], first_back_recv.at[h, k]
+            send(first_out.at[h, k], first_in.at[h, k], *sems, dev, side)
+
+    totals = []
+
+    def to_column(h, k):
+        z = (me_z + k) % columns
+        total = both(h, me_p, z, me_y)
+        for j in range(1, pairs):
+            total = total + second_in[h, j - 1, k, 0].astype(F32)
+        if near == 2:
+            arrive(first_in.at[h, k], first_back_send.at[h, k], first_back_recv.at[h, k])
+            total = total + first_in[h, k].astype(F32)
+        if k == 0:
+            totals.append(total)
+            return
+        column_out[h, k - 1] = total.astype(BF16)
+        dev, side = device(me_p, z, me_y)
+        sems = column_back_send.at[h, k - 1], column_back_recv.at[h, k - 1]
+        send(column_out.at[h, k - 1], column_in.at[h, k - 1], *sems, dev, side)
+
+    for i in range(len(steps) + 2):
+        if i < len(steps):
+            to_first(*steps[i])
+        if i >= 2:
+            to_column(*steps[i - 2])
+    for h in range(2):
+        total = totals[h]
+        for k in range(1, columns):
+            sems = column_back_send.at[h, k - 1], column_back_recv.at[h, k - 1]
+            arrive(column_in.at[h, k - 1], *sems)
+            total = total + column_in[h, k - 1].astype(F32)
+        sum_ref[:, h * half : (h + 1) * half] = total.astype(BF16)
     for copy in sent:
         copy.wait_send()
-
-
-def hand_out(stream_ref, sum_ref, stream_out, sum_out, sem):
-    copies = [
-        pltpu.make_async_copy(stream_ref, stream_out, sem.at[0]),
-        pltpu.make_async_copy(sum_ref, sum_out, sem.at[1]),
-    ]
-    for copy in copies:
-        copy.start()
-    for copy in copies:
-        copy.wait()
 
 
 def body(
@@ -370,8 +434,8 @@
     pairs = sides // 2
     rows, width = residual.shape
     heads = queries.shape[1] // HD
-    units = w_down.shape[1]
-    tokens = devs * 2 * rows
+    near = 2 if devs % 2 == 0 else 1
+    columns, half = devs // near, width // 2
     dma = pltpu.SemaphoreType.DMA
     vmem = pl.BlockSpec(memory_space=pltpu.VMEM)
     hbm = pl.BlockSpec(memory_space=pl.ANY)
@@ -380,8 +444,8 @@
     results = pl.pallas_call(
         functools.partial(kernel, devs, sides),
         out_shape=(
-            jax.ShapeDtypeStruct((rows, width), BF16),
-            jax.ShapeDtypeStruct((rows, width), BF16),
+            pltpu.VMEM((rows, width), BF16),
+            pltpu.VMEM((rows, width), BF16),
         ),
         in_specs=[pl.BlockSpec(memory_space=pltpu.SMEM)] + [hbm] * 10,
         out_specs=(vmem, vmem),
@@ -397,34 +461,28 @@
             pltpu.VMEM((sides, rows, width), BF16),
             pltpu.VMEM((sides - 1, rows, width), BF16),
             pltpu.VMEM((sides, rows, width), F32),
-            pltpu.VMEM((pairs, devs, 2, rows, width + LANES), BF16),
-            pltpu.VMEM((pairs, tokens, units), BF16),
-            pltpu.VMEM((pairs, devs, rows, width), BF16),
-            pltpu.VMEM((pairs, devs, rows, width), BF16),
-            pltpu.VMEM((pairs, devs, rows, width), F32),
-            pltpu.VMEM((max(1, pairs - 1), devs, rows, width), BF16),
-            pltpu.VMEM((max(1, pairs - 1), devs, rows, width), BF16),
-            pltpu.VMEM((devs - 1, rows, width), BF16),
-            pltpu.VMEM((devs - 1, rows, width), BF16),
+            pltpu.VMEM((pairs, columns, near, 2, rows, width + LANES), BF16),
+            pltpu.VMEM((2, pairs, columns, near, rows, half), BF16),
+            pltpu.VMEM((2, pairs, columns, near, rows, half), BF16),
+            pltpu.VMEM((2, pairs, columns, near, rows, half), F32),
+            pltpu.VMEM((2, max(1, pairs - 1), columns, near, rows, half), BF16),
+            pltpu.VMEM((2, max(1, pairs - 1), columns, near, rows, half), BF16),
+            pltpu.VMEM((2, columns, rows, half), BF16),
+            pltpu.VMEM((2, columns, rows, half), BF16),
+            pltpu.VMEM((2, max(1, columns - 1), rows, half), BF16),
+            pltpu.VMEM((2, max(1, columns - 1), rows, half), BF16),
             dma((len(small),)),
             dma((rows,)),
             dma((3,)),
-            dma((sides - 1,)),
-            dma((sides - 1,)),
-            dma((sides - 1,)),
-            dma((sides - 1,)),
-            dma((devs - 1,)),
-            dma((devs - 1,)),
-            dma((max(1, pairs - 1), devs)),
-            dma((max(1, pairs - 1), devs)),
-            dma((pairs, devs)),
-            dma((pairs, devs)),
-            dma((pairs,)),
-            dma((pairs,)),
-            dma((max(1, pairs - 1), devs)),
-            dma((max(1, pairs - 1), devs)),
-            dma((devs - 1,)),
-            dma((devs - 1,)),
+            *[dma((sides - 1,))] * 4,
+            *[dma((max(1, columns - 1),))] * 2,
+            *[dma((columns,))] * 2,
+            *[dma((max(1, pairs - 1), columns, near))] * 2,
+            *[dma((pairs, columns, near))] * 2,
+            *[dma((2,))] * 2,
+            *[dma((2, max(1, pairs - 1), columns))] * 2,
+            *[dma((2, columns))] * 2,
+            *[dma((2, max(1, columns - 1)))] * 2,
         ],
         compiler_params=pltpu.CompilerParams(
             collective_id=0, has_side_effects=True, vmem_limit_bytes=56 * 1024 * 1024
@@ -437,14 +495,7 @@
         w_in,
         w_down,
     )
-    return pl.pallas_call(
-        hand_out,
-        out_shape=tuple(jax.ShapeDtypeStruct((rows, width), BF16) for _ in results),
-        in_specs=[hbm] * 2,
-        out_specs=(hbm, hbm),
-        scratch_shapes=[dma((2,))],
-        compiler_params=pltpu.CompilerParams(vmem_limit_bytes=56 * 1024 * 1024),
-    )(*results)
+    return results
 
 
 def solution(mesh):

time: 45.9 us -> 49.1 us (1.070)
  Pallas kernels: 45.1 us -> 47.1 us
  local copies, waits for them, and re-layouts: 0 us -> 1.23 us
    pallas_call x2 -> x1, Pallas kernels: 45.1 us -> 47.1 us  [body(): pl.pallas_call(functools.partial(kernel, devs, sides), out_shape=(pltpu.V...]
    unnamed x0 -> x2, local copies, waits for them, and re-layouts: none -> 1.23 us
where the time goes in v3:
time: 49.1 us; the launch traced here: 49 us
  Pallas kernels  47.1 us (96%)
  local copies, waits for them, and re-layouts  1.23 us (3%)
  between operations  0.64 us (1%)
    pallas_call x1, Pallas kernels, body(): pl.pallas_call(functools.partial(kernel, devs, sides), out_shape=(pltpu.V...  47.1 us
    unnamed x2, local copies, waits for them, and re-layouts  1.23 us

profile of v3, /device:TPU:0, one launch (start us, length us, event | category | flops | bytes accessed | tf_op | source)
XLA Modules:
  0.0 49.0 jit_solution(8826327178710205983)
XLA Ops:
  0.6 47.1 %shard_map.122 = (bf16[8,2048]{1,0:T(8,128)(2,1)S(1)}, bf16[8,2048]{1,0:T(8,128)(2,1)S(1)}) custom-call(s32[8]{0:T(128)} %lengths_ref.1, bf16[8,4096]{1,0:T(8,128)(2,1)} %queries_hbm.1, bf16[8,1024]{1,0:T(8,128)(2,1)} %new_kv_hbm.1, bf16[8,2048]{1,0:T(8,128)(2,1)} %residual_hbm.1, f32[1,2048]{1,0:T(1,128)} %bitcast.1, s32[8,8]{1,0:T(8,128)} %ids_hbm.1, ...), custom_call_target="tpu_custom_call" | custom-call | tf_op jit(solution)/shard_map/pallas_call | solution.py:444
  47.8 0.6 %copy.15 = bf16[8,2048]{1,0:T(8,128)(2,1)} copy(bf16[8,2048]{1,0:T(8,128)(2,1)S(1)} %get-tuple-element.2) | data formatting | bytes 65536
  48.4 0.6 %copy.16 = bf16[8,2048]{1,0:T(8,128)(2,1)} copy(bf16[8,2048]{1,0:T(8,128)(2,1)S(1)} %get-tuple-element.3) | data formatting | bytes 65536

commit v4 on v2

--- a/solution.py
+++ b/solution.py
@@ -48,7 +48,6 @@
     part_in,
     part_own,
     gathered,
-    hidden,
     half_out,
     half_in,
     half_own,
@@ -221,7 +220,7 @@
     spread = jnp.zeros((rows, LANES), F32)
     for k in range(ids.shape[1]):
         spread = spread + jnp.where(ids[:, k : k + 1] == expert_lane, levels[:, k : k + 1], 0.0)
-    gathered[me_p, me_d, me_c, :, width:] = spread.astype(BF16)
+    gathered[0, 0, me_c, :, width:] = spread.astype(BF16)
     out_copy.wait()
     for k in range(1, sides):
         arrive(mixed_in.at[(me_s + sides - k) % sides], mixed_send.at[k - 1], mixed_recv.at[k - 1])
@@ -239,118 +238,113 @@
         stream = stream + part_in[k - 1].astype(F32)
     mean_square = jnp.mean(stream * stream, axis=1, keepdims=True)
     normed = stream * lax.rsqrt(mean_square + 1e-06) * gain_ref[...]
-    gathered[me_p, me_d, me_c, :, :width] = normed.astype(BF16)
-
-    def share(j, k, block):
-        send(block, block, sib_send.at[j, k], sib_recv.at[j, k], me_d, sib_s)
-
-    def across(k, block):
+    gathered[0, 0, me_c, :, :width] = normed.astype(BF16)
+
+    def share(k, j):
+        block = gathered.at[k, j, me_c]
+        send(block, block, sib_send.at[k, j], sib_recv.at[k, j], me_d, sib_s)
+
+    def across(k):
         for j in range(1, pairs):
             to = 2 * ((me_p + j) % pairs) + me_c
-            send(block, block, across_send.at[j - 1, k], across_recv.at[j - 1, k], me_d, to)
-
-    mine = gathered.at[me_p, me_d, me_c]
+            sems = across_send.at[k, j - 1], across_recv.at[k, j - 1]
+            send(gathered.at[k, 0, me_c], gathered.at[k, j, me_c], *sems, me_d, to)
+
+    def from_across(k):
+        for j in range(1, pairs):
+            arrive(gathered.at[k, j, me_c], across_send.at[k, j - 1], across_recv.at[k, j - 1])
+            share(k, j)
+
     for k in range(1, devs):
-        send(mine, mine, dev_send.at[k - 1], dev_recv.at[k - 1], (me_d + k) % devs, me_s)
-    across(0, mine)
-    share(0, 0, mine)
+        sems = dev_send.at[k - 1], dev_recv.at[k - 1]
+        dev = (me_d + k) % devs
+        send(gathered.at[0, 0, me_c], gathered.at[k, 0, me_c], *sems, dev, me_s)
+    across(0)
+    share(0, 0)
     stream_ref[...] = stream.astype(BF16)
+    lag = 2
     for k in range(1, devs):
-        block = gathered.at[me_p, (me_d + devs - k) % devs, me_c]
-        arrive(block, dev_send.at[k - 1], dev_recv.at[k - 1])
-        across(k, block)
-        share(0, k, block)
-
-    def from_sibling(j):
-        for k in range(devs):
-            block = gathered.at[(me_p + pairs - j) % pairs, (me_d + devs - k) % devs, 1 - me_c]
-            arrive(block, sib_send.at[j, k], sib_recv.at[j, k])
-
-    tokens = devs * 2 * rows
+        arrive(gathered.at[k, 0, me_c], dev_send.at[k - 1], dev_recv.at[k - 1])
+        across(k)
+        share(k, 0)
+        if k >= lag:
+            from_across(k - lag)
+
     expert = me_d * pairs + me_p
-    token_lane = lax.broadcasted_iota(jnp.int32, (tokens, LANES), 1)
-
-    def first_half(j):
-        block = gathered[(me_p + pairs - j) % pairs].astype(F32).reshape(tokens, width + LANES)
+    ranges = [r for r in ((0, devs // 2), (devs // 2, devs)) if r[0] < r[1]]
+
+    def first_half(first, last):
+        for k in range(first, last):
+            for j in range(pairs):
+                arrive(gathered.at[k, j, 1 - me_c], sib_send.at[k, j], sib_recv.at[k, j])
+        tokens = (last - first) * pairs * 2 * rows
+        block = gathered[first:last].astype(F32).reshape(tokens, width + LANES)
+        level = block[:, width:]
+        token_lane = lax.broadcasted_iota(jnp.int32, (tokens, LANES), 1)
+        chosen = jnp.sum(jnp.where(token_lane == expert, level, 0.0), axis=1, keepdims=True)
+        weight = chosen / jnp.sum(level, axis=1, keepdims=True)
         gate_up = jnp.dot(block[:, :width].astype(BF16), w_in[...], preferred_element_type=F32)
         gate = gate_up[:, :units]
-        hidden[j] = (gate / (1.0 + jnp.exp(-gate)) * gate_up[:, units:]).astype(BF16)
-
-    def second_half(j):
-        level = gathered[(me_p + pairs - j) % pairs, :, :, :, width:].astype(F32)
-        level = level.reshape(tokens, LANES)
-        chosen = jnp.sum(jnp.where(token_lane == expert, level, 0.0), axis=1, keepdims=True)
-        weight = chosen / jnp.sum(level, axis=1, keepdims=True)
-        out = jnp.dot(hidden[j], w_down[...], preferred_element_type=F32) * weight
-        out = out.reshape(devs, 2, rows, width)
-        half_own[j] = jnp.where(me_c == 0, out[:, 0], out[:, 1])
-        half_out[j] = jnp.where(me_c == 0, out[:, 1], out[:, 0]).astype(BF16)
-        send(half_out.at[j], half_in.at[j], half_send.at[j], half_recv.at[j], me_d, sib_s)
+        return (gate / (1.0 + jnp.exp(-gate)) * gate_up[:, units:]).astype(BF16), weight
+
+    def second_half(i, first, last, hidden, weight):
+        out = jnp.dot(hidden, w_down[...], preferred_element_type=F32) * weight
+        out = out.reshape(last - first, pairs, 2, rows, width)
+        half_own[first:last] = jnp.where(me_c == 0, out[:, :, 0], out[:, :, 1])
+        half_out[first:last] = jnp.where(me_c == 0, out[:, :, 1], out[:, :, 0]).astype(BF16)
+        sems = half_send.at[i], half_recv.at[i]
+        send(half_out.at[first:last], half_in.at[first:last], *sems, me_d, sib_s)
+
+    def back_across(i, first, last):
+        arrive(half_in.at[first:last], half_send.at[i], half_recv.at[i])
+        for k in order(first, last):
+            for j in range(1, pairs):
+                to = 2 * ((me_p + pairs - j) % pairs) + me_c
+                pair_out[k, j - 1] = (half_own[k, j] + half_in[k, j].astype(F32)).astype(BF16)
+                sems = pair_send.at[k, j - 1], pair_recv.at[k, j - 1]
+                send(pair_out.at[k, j - 1], pair_in.at[k, j - 1], *sems, me_d, to)
+
+    def order(first, last):
+        return [k for k in range(first, last) if k > 0] + ([0] if first == 0 else [])
+
+    kept = []
+
+    def back_along(first, last):
+        for k in order(first, last):
+            total = half_own[k, 0] + half_in[k, 0].astype(F32)
+            for j in range(1, pairs):
+                arrive(pair_in.at[k, j - 1], pair_send.at[k, j - 1], pair_recv.at[k, j - 1])
+                total = total + pair_in[k, j - 1].astype(F32)
+            if k == 0:
+                kept.append(total)
+                continue
+            last_out[k - 1] = total.astype(BF16)
+            sems = last_send.at[k - 1], last_recv.at[k - 1]
+            dev = (me_d + devs - k) % devs
+            send(last_out.at[k - 1], last_in.at[k - 1], *sems, dev, me_s)
 
     in_copy.wait()
-    from_sibling(0)
-    first_half(0)
-    for j in range(1, pairs):
-        for k in range(devs):
-            block = gathered.at[(me_p + pairs - j) % pairs, (me_d + devs - k) % devs, me_c]
-            arrive(block, across_send.at[j - 1, k], across_recv.at[j - 1, k])
-            share(j, k, block)
+    early = first_half(*ranges[0]) if len(ranges) > 1 else None
+    for k in range(max(0, devs - lag), devs):
+        from_across(k)
     down_copy.wait()
-    for j in range(1, pairs):
-        from_sibling(j)
-        first_half(j)
-        second_half(j)
-    second_half(0)
-
-    for j in range(1, pairs):
-        arrive(half_in.at[j], half_send.at[j], half_recv.at[j])
-        to = 2 * ((me_p + pairs - j) % pairs) + me_c
-        for k in range(1, devs + 1):
-            dev = (me_d + k) % devs
-            pair_out[j - 1, dev] = (half_own[j, dev] + half_in[j, dev].astype(F32)).astype(BF16)
-            send(
-                pair_out.at[j - 1, dev],
-                pair_in.at[j - 1, dev],
-                pair_send.at[j - 1, k - 1],
-                pair_recv.at[j - 1, k - 1],
-                me_d,
-                to,
-            )
-    arrive(half_in.at[0], half_send.at[0], half_recv.at[0])
-    total = None
-    for k in range(1, devs + 1):
-        dev = (me_d + k) % devs
-        total = half_own[0, dev] + half_in[0, dev].astype(F32)
-        for j in range(1, pairs):
-            arrive(pair_in.at[j - 1, dev], pair_send.at[j - 1, k - 1], pair_recv.at[j - 1, k - 1])
-            total = total + pair_in[j - 1, dev].astype(F32)
-        if k < devs:
-            last_out[k - 1] = total.astype(BF16)
-            send(
-                last_out.at[k - 1],
-                last_in.at[k - 1],
-                last_send.at[k - 1],
-                last_recv.at[k - 1],
-                dev,
-                me_s,
-            )
+    if early is not None:
+        second_half(0, *ranges[0], *early)
+    late = first_half(*ranges[-1])
+    if early is not None:
+        back_across(0, *ranges[0])
+    second_half(len(ranges) - 1, *ranges[-1], *late)
+    if early is not None:
+        back_along(*ranges[0])
+    back_across(len(ranges) - 1, *ranges[-1])
+    back_along(*ranges[-1])
+    total = kept[0]
     for k in range(1, devs):
         arrive(last_in.at[k - 1], last_send.at[k - 1], last_recv.at[k - 1])
         total = total + last_in[k - 1].astype(F32)
     sum_ref[...] = total.astype(BF16)
     for copy in sent:
         copy.wait_send()
-
-
-def hand_out(stream_ref, sum_ref, stream_out, sum_out, sem):
-    copies = [
-        pltpu.make_async_copy(stream_ref, stream_out, sem.at[0]),
-        pltpu.make_async_copy(sum_ref, sum_out, sem.at[1]),
-    ]
-    for copy in copies:
-        copy.start()
-    for copy in copies:
-        copy.wait()
 
 
 def body(
@@ -370,18 +364,16 @@
     pairs = sides // 2
     rows, width = residual.shape
     heads = queries.shape[1] // HD
-    units = w_down.shape[1]
-    tokens = devs * 2 * rows
     dma = pltpu.SemaphoreType.DMA
     vmem = pl.BlockSpec(memory_space=pltpu.VMEM)
     hbm = pl.BlockSpec(memory_space=pl.ANY)
     norm_gain = norm_gain.reshape(1, -1)
     small = (queries, new_kv, residual, norm_gain, expert_ids, route_level)
-    results = pl.pallas_call(
+    return pl.pallas_call(
         functools.partial(kernel, devs, sides),
         out_shape=(
-            jax.ShapeDtypeStruct((rows, width), BF16),
-            jax.ShapeDtypeStruct((rows, width), BF16),
+            pltpu.VMEM((rows, width), BF16),
+            pltpu.VMEM((rows, width), BF16),
         ),
         in_specs=[pl.BlockSpec(memory_space=pltpu.SMEM)] + [hbm] * 10,
         out_specs=(vmem, vmem),
@@ -397,34 +389,24 @@
             pltpu.VMEM((sides, rows, width), BF16),
             pltpu.VMEM((sides - 1, rows, width), BF16),
             pltpu.VMEM((sides, rows, width), F32),
-            pltpu.VMEM((pairs, devs, 2, rows, width + LANES), BF16),
-            pltpu.VMEM((pairs, tokens, units), BF16),
-            pltpu.VMEM((pairs, devs, rows, width), BF16),
-            pltpu.VMEM((pairs, devs, rows, width), BF16),
-            pltpu.VMEM((pairs, devs, rows, width), F32),
-            pltpu.VMEM((max(1, pairs - 1), devs, rows, width), BF16),
-            pltpu.VMEM((max(1, pairs - 1), devs, rows, width), BF16),
+            pltpu.VMEM((devs, pairs, 2, rows, width + LANES), BF16),
+            pltpu.VMEM((devs, pairs, rows, width), BF16),
+            pltpu.VMEM((devs, pairs, rows, width), BF16),
+            pltpu.VMEM((devs, pairs, rows, width), F32),
+            pltpu.VMEM((devs, max(1, pairs - 1), rows, width), BF16),
+            pltpu.VMEM((devs, max(1, pairs - 1), rows, width), BF16),
             pltpu.VMEM((devs - 1, rows, width), BF16),
             pltpu.VMEM((devs - 1, rows, width), BF16),
             dma((len(small),)),
             dma((rows,)),
             dma((3,)),
-            dma((sides - 1,)),
-            dma((sides - 1,)),
-            dma((sides - 1,)),
-            dma((sides - 1,)),
-            dma((devs - 1,)),
-            dma((devs - 1,)),
-            dma((max(1, pairs - 1), devs)),
-            dma((max(1, pairs - 1), devs)),
-            dma((pairs, devs)),
-            dma((pairs, devs)),
-            dma((pairs,)),
-            dma((pairs,)),
-            dma((max(1, pairs - 1), devs)),
-            dma((max(1, pairs - 1), devs)),
-            dma((devs - 1,)),
-            dma((devs - 1,)),
+            *[dma((sides - 1,))] * 4,
+            *[dma((devs - 1,))] * 2,
+            *[dma((devs, max(1, pairs - 1)))] * 2,
+            *[dma((devs, pairs))] * 2,
+            *[dma((2,))] * 2,
+            *[dma((devs, max(1, pairs - 1)))] * 2,
+            *[dma((devs - 1,))] * 2,
         ],
         compiler_params=pltpu.CompilerParams(
             collective_id=0, has_side_effects=True, vmem_limit_bytes=56 * 1024 * 1024
@@ -437,14 +419,6 @@
         w_in,
         w_down,
     )
-    return pl.pallas_call(
-        hand_out,
-        out_shape=tuple(jax.ShapeDtypeStruct((rows, width), BF16) for _ in results),
-        in_specs=[hbm] * 2,
-        out_specs=(hbm, hbm),
-        scratch_shapes=[dma((2,))],
-        compiler_params=pltpu.CompilerParams(vmem_limit_bytes=56 * 1024 * 1024),
-    )(*results)
 
 
 def solution(mesh):

time: 45.9 us -> 48.5 us (1.057)
  Pallas kernels: 45.1 us -> 46.4 us
  local copies, waits for them, and re-layouts: 0 us -> 1.23 us
    pallas_call x2 -> x1, Pallas kernels: 45.1 us -> 46.4 us  [body(): pl.pallas_call(functools.partial(kernel, devs, sides), out_shape=(pltpu.V...]
    unnamed x0 -> x2, local copies, waits for them, and re-layouts: none -> 1.23 us
where the time goes in v4:
time: 48.5 us; the launch traced here: 48.3 us
  Pallas kernels  46.4 us (96%)
  local copies, waits for them, and re-layouts  1.23 us (3%)
  between operations  0.64 us (1%)
    pallas_call x1, Pallas kernels, body(): pl.pallas_call(functools.partial(kernel, devs, sides), out_shape=(pltpu.V...  46.4 us
    unnamed x2, local copies, waits for them, and re-layouts  1.23 us

profile of v4, /device:TPU:0, one launch (start us, length us, event | category | flops | bytes accessed | tf_op | source)
XLA Modules:
  0.0 48.3 jit_solution(5139215399528391138)
XLA Ops:
  0.6 46.4 %shard_map.122 = (bf16[8,2048]{1,0:T(8,128)(2,1)S(1)}, bf16[8,2048]{1,0:T(8,128)(2,1)S(1)}) custom-call(s32[8]{0:T(128)} %lengths_ref.1, bf16[8,4096]{1,0:T(8,128)(2,1)} %queries_hbm.1, bf16[8,1024]{1,0:T(8,128)(2,1)} %new_kv_hbm.1, bf16[8,2048]{1,0:T(8,128)(2,1)} %residual_hbm.1, f32[1,2048]{1,0:T(1,128)} %bitcast.1, s32[8,8]{1,0:T(8,128)} %ids_hbm.1, ...), custom_call_target="tpu_custom_call" | custom-call | tf_op jit(solution)/shard_map/pallas_call | solution.py:372
  47.1 0.6 %copy.15 = bf16[8,2048]{1,0:T(8,128)(2,1)} copy(bf16[8,2048]{1,0:T(8,128)(2,1)S(1)} %get-tuple-element.2) | data formatting | bytes 65536
  47.7 0.6 %copy.16 = bf16[8,2048]{1,0:T(8,128)(2,1)} copy(bf16[8,2048]{1,0:T(8,128)(2,1)S(1)} %get-tuple-element.3) | data formatting | bytes 65536

commit v5 on v2

--- a/solution.py
+++ b/solution.py
@@ -270,11 +270,20 @@
     expert = me_d * pairs + me_p
     token_lane = lax.broadcasted_iota(jnp.int32, (tokens, LANES), 1)
 
-    def first_half(j):
-        block = gathered[(me_p + pairs - j) % pairs].astype(F32).reshape(tokens, width + LANES)
-        gate_up = jnp.dot(block[:, :width].astype(BF16), w_in[...], preferred_element_type=F32)
-        gate = gate_up[:, :units]
-        hidden[j] = (gate / (1.0 + jnp.exp(-gate)) * gate_up[:, units:]).astype(BF16)
+    def first_half(j, between=()):
+        block = gathered[(me_p + pairs - j) % pairs, :, :, :, :width].astype(F32)
+        block = block.reshape(tokens, width).astype(BF16)
+        step = units // max(1, len(between))
+        for i in range(units // step):
+            cols = slice(i * step, (i + 1) * step)
+            both = jnp.concatenate(
+                [w_in[:, cols], w_in[:, units + i * step : units + (i + 1) * step]], axis=1
+            )
+            gate_up = jnp.dot(block, both, preferred_element_type=F32)
+            gate = gate_up[:, :step]
+            hidden[j, :, cols] = (gate / (1.0 + jnp.exp(-gate)) * gate_up[:, step:]).astype(BF16)
+            if between:
+                from_across(between[i])
 
     def second_half(j):
         level = gathered[(me_p + pairs - j) % pairs, :, :, :, width:].astype(F32)
@@ -287,14 +296,19 @@
         half_out[j] = jnp.where(me_c == 0, out[:, 1], out[:, 0]).astype(BF16)
         send(half_out.at[j], half_in.at[j], half_send.at[j], half_recv.at[j], me_d, sib_s)
 
+    def from_across(ks):
+        for k in ks:
+            for j in range(1, pairs):
+                block = gathered.at[(me_p + pairs - j) % pairs, (me_d + devs - k) % devs, me_c]
+                arrive(block, across_send.at[j - 1, k], across_recv.at[j - 1, k])
+                share(j, k, block)
+
     in_copy.wait()
+    order = list(range(devs))
+    cuts = [order[: devs // 2], order[devs // 2 : devs * 3 // 4], order[devs * 3 // 4 : devs - 1]]
+    from_across(cuts[0])
     from_sibling(0)
-    first_half(0)
-    for j in range(1, pairs):
-        for k in range(devs):
-            block = gathered.at[(me_p + pairs - j) % pairs, (me_d + devs - k) % devs, me_c]
-            arrive(block, across_send.at[j - 1, k], across_recv.at[j - 1, k])
-            share(j, k, block)
+    first_half(0, (cuts[1], cuts[2], order[devs - 1 :]))
     down_copy.wait()
     for j in range(1, pairs):
         from_sibling(j)
@@ -342,17 +356,6 @@
         copy.wait_send()
 
 
-def hand_out(stream_ref, sum_ref, stream_out, sum_out, sem):
-    copies = [
-        pltpu.make_async_copy(stream_ref, stream_out, sem.at[0]),
-        pltpu.make_async_copy(sum_ref, sum_out, sem.at[1]),
-    ]
-    for copy in copies:
-        copy.start()
-    for copy in copies:
-        copy.wait()
-
-
 def body(
     queries,
     kv_cache,
@@ -377,11 +380,11 @@
     hbm = pl.BlockSpec(memory_space=pl.ANY)
     norm_gain = norm_gain.reshape(1, -1)
     small = (queries, new_kv, residual, norm_gain, expert_ids, route_level)
-    results = pl.pallas_call(
+    return pl.pallas_call(
         functools.partial(kernel, devs, sides),
         out_shape=(
-            jax.ShapeDtypeStruct((rows, width), BF16),
-            jax.ShapeDtypeStruct((rows, width), BF16),
+            pltpu.VMEM((rows, width), BF16),
+            pltpu.VMEM((rows, width), BF16),
         ),
         in_specs=[pl.BlockSpec(memory_space=pltpu.SMEM)] + [hbm] * 10,
         out_specs=(vmem, vmem),
@@ -437,14 +440,6 @@
         w_in,
         w_down,
     )
-    return pl.pallas_call(
-        hand_out,
-        out_shape=tuple(jax.ShapeDtypeStruct((rows, width), BF16) for _ in results),
-        in_specs=[hbm] * 2,
-        out_specs=(hbm, hbm),
-        scratch_shapes=[dma((2,))],
-        compiler_params=pltpu.CompilerParams(vmem_limit_bytes=56 * 1024 * 1024),
-    )(*results)
 
 
 def solution(mesh):

time: 45.9 us -> 43.6 us (0.950)
  Pallas kernels: 45.1 us -> 41.5 us
  local copies, waits for them, and re-layouts: 0 us -> 1.23 us
    pallas_call x2 -> x1, Pallas kernels: 45.1 us -> 41.5 us  [body(): pl.pallas_call(functools.partial(kernel, devs, sides), out_shape=(pltpu.V...]
    unnamed x0 -> x2, local copies, waits for them, and re-layouts: none -> 1.23 us
where the time goes in v5:
time: 43.6 us; the launch traced here: 43.4 us
  Pallas kernels  41.5 us (95%)
  local copies, waits for them, and re-layouts  1.23 us (3%)
  between operations  0.64 us (1%)
    pallas_call x1, Pallas kernels, body(): pl.pallas_call(functools.partial(kernel, devs, sides), out_shape=(pltpu.V...  41.5 us
    unnamed x2, local copies, waits for them, and re-layouts  1.23 us

profile of v5, /device:TPU:0, one launch (start us, length us, event | category | flops | bytes accessed | tf_op | source)
XLA Modules:
  0.0 43.4 jit_solution(3207993545433095357)
XLA Ops:
  0.6 41.5 %shard_map.122 = (bf16[8,2048]{1,0:T(8,128)(2,1)S(1)}, bf16[8,2048]{1,0:T(8,128)(2,1)S(1)}) custom-call(s32[8]{0:T(128)} %lengths_ref.1, bf16[8,4096]{1,0:T(8,128)(2,1)} %queries_hbm.1, bf16[8,1024]{1,0:T(8,128)(2,1)} %new_kv_hbm.1, bf16[8,2048]{1,0:T(8,128)(2,1)} %residual_hbm.1, f32[1,2048]{1,0:T(1,128)} %bitcast.1, s32[8,8]{1,0:T(8,128)} %ids_hbm.1, ...), custom_call_target="tpu_custom_call" | custom-call | tf_op jit(solution)/shard_map/pallas_call | solution.py:383
  42.2 0.6 %copy.15 = bf16[8,2048]{1,0:T(8,128)(2,1)} copy(bf16[8,2048]{1,0:T(8,128)(2,1)S(1)} %get-tuple-element.2) | data formatting | bytes 65536
  42.8 0.6 %copy.16 = bf16[8,2048]{1,0:T(8,128)(2,1)} copy(bf16[8,2048]{1,0:T(8,128)(2,1)S(1)} %get-tuple-element.3) | data formatting | bytes 65536

commit v6 on v5

--- a/solution.py
+++ b/solution.py
@@ -285,16 +285,27 @@
             if between:
                 from_across(between[i])
 
-    def second_half(j):
+    half = width // 2
+    halves = (slice(0, half), slice(half, width))
+
+    def second_half(j, c):
         level = gathered[(me_p + pairs - j) % pairs, :, :, :, width:].astype(F32)
         level = level.reshape(tokens, LANES)
         chosen = jnp.sum(jnp.where(token_lane == expert, level, 0.0), axis=1, keepdims=True)
         weight = chosen / jnp.sum(level, axis=1, keepdims=True)
-        out = jnp.dot(hidden[j], w_down[...], preferred_element_type=F32) * weight
-        out = out.reshape(devs, 2, rows, width)
-        half_own[j] = jnp.where(me_c == 0, out[:, 0], out[:, 1])
-        half_out[j] = jnp.where(me_c == 0, out[:, 1], out[:, 0]).astype(BF16)
-        send(half_out.at[j], half_in.at[j], half_send.at[j], half_recv.at[j], me_d, sib_s)
+        out = jnp.dot(hidden[j], w_down[:, halves[c]], preferred_element_type=F32) * weight
+        out = out.reshape(devs, 2, rows, half)
+        half_own[j, c] = jnp.where(me_c == 0, out[:, 0], out[:, 1])
+        half_out[j, c] = jnp.where(me_c == 0, out[:, 1], out[:, 0]).astype(BF16)
+        sems = half_send.at[j, c], half_recv.at[j, c]
+        send(half_out.at[j, c], half_in.at[j, c], *sems, me_d, sib_s)
+
+    def from_half(j):
+        for c in range(2):
+            arrive(half_in.at[j, c], half_send.at[j, c], half_recv.at[j, c])
+
+    def joined(j, c, dev):
+        return half_own[j, c, dev] + half_in[j, c, dev].astype(F32)
 
     def from_across(ks):
         for k in ks:
@@ -313,41 +324,32 @@
     for j in range(1, pairs):
         from_sibling(j)
         first_half(j)
-        second_half(j)
-    second_half(0)
+        second_half(j, 0)
+        second_half(j, 1)
+    second_half(0, 0)
 
     for j in range(1, pairs):
-        arrive(half_in.at[j], half_send.at[j], half_recv.at[j])
+        from_half(j)
         to = 2 * ((me_p + pairs - j) % pairs) + me_c
         for k in range(1, devs + 1):
             dev = (me_d + k) % devs
-            pair_out[j - 1, dev] = (half_own[j, dev] + half_in[j, dev].astype(F32)).astype(BF16)
-            send(
-                pair_out.at[j - 1, dev],
-                pair_in.at[j - 1, dev],
-                pair_send.at[j - 1, k - 1],
-                pair_recv.at[j - 1, k - 1],
-                me_d,
-                to,
-            )
-    arrive(half_in.at[0], half_send.at[0], half_recv.at[0])
+            for c in range(2):
+                pair_out[j - 1, dev, :, halves[c]] = joined(j, c, dev).astype(BF16)
+            sems = pair_send.at[j - 1, k - 1], pair_recv.at[j - 1, k - 1]
+            send(pair_out.at[j - 1, dev], pair_in.at[j - 1, dev], *sems, me_d, to)
+    second_half(0, 1)
+    from_half(0)
     total = None
     for k in range(1, devs + 1):
         dev = (me_d + k) % devs
-        total = half_own[0, dev] + half_in[0, dev].astype(F32)
+        total = jnp.concatenate([joined(0, c, dev) for c in range(2)], axis=1)
         for j in range(1, pairs):
             arrive(pair_in.at[j - 1, dev], pair_send.at[j - 1, k - 1], pair_recv.at[j - 1, k - 1])
             total = total + pair_in[j - 1, dev].astype(F32)
         if k < devs:
             last_out[k - 1] = total.astype(BF16)
-            send(
-                last_out.at[k - 1],
-                last_in.at[k - 1],
-                last_send.at[k - 1],
-                last_recv.at[k - 1],
-                dev,
-                me_s,
-            )
+            sems = last_send.at[k - 1], last_recv.at[k - 1]
+            send(last_out.at[k - 1], last_in.at[k - 1], *sems, dev, me_s)
     for k in range(1, devs):
         arrive(last_in.at[k - 1], last_send.at[k - 1], last_recv.at[k - 1])
         total = total + last_in[k - 1].astype(F32)
@@ -402,9 +404,9 @@
             pltpu.VMEM((sides, rows, width), F32),
             pltpu.VMEM((pairs, devs, 2, rows, width + LANES), BF16),
             pltpu.VMEM((pairs, tokens, units), BF16),
-            pltpu.VMEM((pairs, devs, rows, width), BF16),
-            pltpu.VMEM((pairs, devs, rows, width), BF16),
-            pltpu.VMEM((pairs, devs, rows, width), F32),
+            pltpu.VMEM((pairs, 2, devs, rows, width // 2), BF16),
+            pltpu.VMEM((pairs, 2, devs, rows, width // 2), BF16),
+            pltpu.VMEM((pairs, 2, devs, rows, width // 2), F32),
             pltpu.VMEM((max(1, pairs - 1), devs, rows, width), BF16),
             pltpu.VMEM((max(1, pairs - 1), devs, rows, width), BF16),
             pltpu.VMEM((devs - 1, rows, width), BF16),
@@ -422,8 +424,8 @@
             dma((max(1, pairs - 1), devs)),
             dma((pairs, devs)),
             dma((pairs, devs)),
-            dma((pairs,)),
-            dma((pairs,)),
+            dma((pairs, 2)),
+            dma((pairs, 2)),
             dma((max(1, pairs - 1), devs)),
             dma((max(1, pairs - 1), devs)),
             dma((devs - 1,)),

time: 43.6 us -> 43.7 us (level)
  no operation moved by 1% of the time
where the time goes in v6:
time: 43.7 us; the launch traced here: 43.5 us
  Pallas kernels  41.7 us (95%)
  local copies, waits for them, and re-layouts  1.23 us (3%)
  between operations  0.64 us (1%)
    pallas_call x1, Pallas kernels, body(): pl.pallas_call(functools.partial(kernel, devs, sides), out_shape=(pltpu.V...  41.7 us
    unnamed x2, local copies, waits for them, and re-layouts  1.23 us

profile of v6, /device:TPU:0, one launch (start us, length us, event | category | flops | bytes accessed | tf_op | source)
XLA Modules:
  0.0 43.5 jit_solution(9533222548765080686)
XLA Ops:
  0.6 41.7 %shard_map.122 = (bf16[8,2048]{1,0:T(8,128)(2,1)S(1)}, bf16[8,2048]{1,0:T(8,128)(2,1)S(1)}) custom-call(s32[8]{0:T(128)} %lengths_ref.1, bf16[8,4096]{1,0:T(8,128)(2,1)} %queries_hbm.1, bf16[8,1024]{1,0:T(8,128)(2,1)} %new_kv_hbm.1, bf16[8,2048]{1,0:T(8,128)(2,1)} %residual_hbm.1, f32[1,2048]{1,0:T(1,128)} %bitcast.1, s32[8,8]{1,0:T(8,128)} %ids_hbm.1, ...), custom_call_target="tpu_custom_call" | custom-call | tf_op jit(solution)/shard_map/pallas_call | solution.py:385
  42.3 0.6 %copy.15 = bf16[8,2048]{1,0:T(8,128)(2,1)} copy(bf16[8,2048]{1,0:T(8,128)(2,1)S(1)} %get-tuple-element.2) | data formatting | bytes 65536
  42.9 0.6 %copy.16 = bf16[8,2048]{1,0:T(8,128)(2,1)} copy(bf16[8,2048]{1,0:T(8,128)(2,1)S(1)} %get-tuple-element.3) | data formatting | bytes 65536

commit v7 on v5

--- a/solution.py
+++ b/solution.py
@@ -316,10 +316,11 @@
         second_half(j)
     second_half(0)
 
+    far_first = sorted(range(1, devs), key=lambda k: -min(k, devs - k)) + [devs]
     for j in range(1, pairs):
         arrive(half_in.at[j], half_send.at[j], half_recv.at[j])
         to = 2 * ((me_p + pairs - j) % pairs) + me_c
-        for k in range(1, devs + 1):
+        for k in far_first:
             dev = (me_d + k) % devs
             pair_out[j - 1, dev] = (half_own[j, dev] + half_in[j, dev].astype(F32)).astype(BF16)
             send(
@@ -332,7 +333,7 @@
             )
     arrive(half_in.at[0], half_send.at[0], half_recv.at[0])
     total = None
-    for k in range(1, devs + 1):
+    for k in far_first:
         dev = (me_d + k) % devs
         total = half_own[0, dev] + half_in[0, dev].astype(F32)
         for j in range(1, pairs):

time: 43.6 us -> 45.1 us (1.034)
  Pallas kernels: 41.5 us -> 43.1 us
    pallas_call x1, Pallas kernels: 41.5 us -> 43.1 us  [body(): pl.pallas_call(functools.partial(kernel, devs, sides), out_shape=(pltpu.V...]
where the time goes in v7:
time: 45.1 us; the launch traced here: 44.9 us
  Pallas kernels  43.1 us (96%)
  local copies, waits for them, and re-layouts  1.23 us (3%)
  between operations  0.64 us (1%)
    pallas_call x1, Pallas kernels, body(): pl.pallas_call(functools.partial(kernel, devs, sides), out_shape=(pltpu.V...  43.1 us
    unnamed x2, local copies, waits for them, and re-layouts  1.23 us

profile of v7, /device:TPU:0, one launch (start us, length us, event | category | flops | bytes accessed | tf_op | source)
XLA Modules:
  0.0 44.9 jit_solution(15632390573342342466)
XLA Ops:
  0.6 43.1 %shard_map.122 = (bf16[8,2048]{1,0:T(8,128)(2,1)S(1)}, bf16[8,2048]{1,0:T(8,128)(2,1)S(1)}) custom-call(s32[8]{0:T(128)} %lengths_ref.1, bf16[8,4096]{1,0:T(8,128)(2,1)} %queries_hbm.1, bf16[8,1024]{1,0:T(8,128)(2,1)} %new_kv_hbm.1, bf16[8,2048]{1,0:T(8,128)(2,1)} %residual_hbm.1, f32[1,2048]{1,0:T(1,128)} %bitcast.1, s32[8,8]{1,0:T(8,128)} %ids_hbm.1, ...), custom_call_target="tpu_custom_call" | custom-call | tf_op jit(solution)/shard_map/pallas_call | solution.py:384
  43.7 0.6 %copy.15 = bf16[8,2048]{1,0:T(8,128)(2,1)} copy(bf16[8,2048]{1,0:T(8,128)(2,1)S(1)} %get-tuple-element.2) | data formatting | bytes 65536
  44.3 0.6 %copy.16 = bf16[8,2048]{1,0:T(8,128)(2,1)} copy(bf16[8,2048]{1,0:T(8,128)(2,1)S(1)} %get-tuple-element.3) | data formatting | bytes 65536
